TPU v7x, 512 devices: a whole 4x4x16 slice. The times are simulated.
512 devices in a mesh: rep: 64 (over z, y), loop: 8 (over x, core).
Axes of the slice: x: 4, y: 4, z: 16, core: 2. Of those that a mesh axis runs over, the one named last changes fastest.
Arguments:
- features: bfloat16 [65536, 256], P(('rep', 'loop')), may hold values from -6 to 6
- tiles: bfloat16 [49152, 128, 128], P(('rep', 'loop'))
- tile_dst: int32 [49152], P(('rep', 'loop')), may hold values from 0 to 7
- tile_src: int32 [49152], P(('rep', 'loop')), may hold values from 0 to 63
- tile_count: int32 [512], P(('rep', 'loop')), may hold values from 24 to 96, as said below
- weights: bfloat16 [2, 256, 256], replicated, may hold values from -0.375 to 0.375
- biases: float32 [2, 256], replicated, may hold values from -3 to 3
Outputs:
- hidden_out: bfloat16 [65536, 256], P(('rep', 'loop'))
Inputs may be any that keep to these rules, and one draw needn't show every extreme that they name: `tile_count`: some device in every draw has all 96 slots occupied.
All inputs are finite; a program needn't handle non-finite values.
Results may differ from a plain program's by a relative error of at most 0.019.
Values may be sent and summed in bfloat16 or wider, within the bound.
A program may use at most 64 MiB of HBM per device.

v0:
```python
import jax
import jax.numpy as jnp
from jax import lax
from jax.sharding import PartitionSpec as P


def sparse_product(gathered, tiles, tile_dst, tile_src, tile_count, nloop):
    block = tiles.shape[1]
    width = gathered.shape[1]
    blocks = gathered.reshape(-1, block, width)
    slot_total = tiles.shape[0]
    group = 16
    lanes = jnp.arange(nloop, dtype=jnp.int32)
    occupied = tile_count[0]

    def accumulate(index, total):
        start = index * group
        tile_group = lax.dynamic_slice_in_dim(tiles, start, group, 0)
        dst_group = lax.dynamic_slice_in_dim(tile_dst, start, group, 0)
        src_group = lax.dynamic_slice_in_dim(tile_src, start, group, 0)
        valid = start + jnp.arange(group, dtype=jnp.int32) < occupied
        src_rows = blocks[src_group]
        products = jnp.einsum(
            "tab,tbf->taf", tile_group, src_rows, preferred_element_type=jnp.float32
        )
        select = ((dst_group[:, None] == lanes[None, :]) & valid[:, None]).astype(jnp.float32)
        return total + jnp.einsum("tj,taf->jaf", select, products)

    initial = jnp.zeros((nloop, block, width), jnp.float32)
    total = lax.fori_loop(0, slot_total // group, accumulate, initial)
    return total.reshape(nloop * block, width)


def one_layer(hidden, tiles, tile_dst, tile_src, tile_count, weight, bias):
    nloop = lax.axis_size("loop")
    gathered = lax.all_gather(hidden, "rep", axis=0, tiled=True)
    partial_value = sparse_product(gathered, tiles, tile_dst, tile_src, tile_count, nloop)
    summed = lax.psum_scatter(partial_value, "loop", scatter_dimension=0, tiled=True)
    aggregate = summed.astype(jnp.bfloat16)
    mixed = jnp.dot(aggregate, weight, preferred_element_type=jnp.float32) + bias[None, :]
    return jax.nn.relu(mixed).astype(jnp.bfloat16)


def body(features, tiles, tile_dst, tile_src, tile_count, weights, biases):
    hidden = features
    for layer in range(weights.shape[0]):
        hidden = one_layer(
            hidden, tiles, tile_dst, tile_src, tile_count, weights[layer], biases[layer]
        )
    return hidden


def solution(mesh):
    in_specs = (
        P(("rep", "loop"), None),
        P(("rep", "loop"), None, None),
        P(("rep", "loop")),
        P(("rep", "loop")),
        P(("rep", "loop")),
        P(),
        P(),
    )
    out_specs = P(("rep", "loop"), None)
    return jax.shard_map(body, mesh=mesh, in_specs=in_specs, out_specs=out_specs, check_vma=False)
```

profile of v0, /device:TPU:1, one launch (start us, length us, event | category | flops | bytes accessed | tf_op | source)
XLA Modules:
  0.0 463.2 jit_solution(16486521773487141479)
XLA Ops:
  7.3 146.8 %all-gather.3.cloned.1.call-done = bf16[8192,256]{1,0:T(8,128)(2,1)} async-done(((bf16[128,256]{1,0:T(8,128)(2,1)}), bf16[8192,256]{1,0:T(8,128)(2,1)}) %all-gather.3.cloned.1.call-update) | async-done | bytes 4194320 | tf_op jit(solution)/shard_map/all_gather | solution.py:36
  154.1 39.4 %while.28 = (s32[]{:T(128)}, f32[8,128,256]{2,0,1:T(8,128)S(1)}, s32[96]{0:T(128)}, s32[]{:T(128)}, bf16[96,128,128]{2,1,0:T(8,128)(2,1)}, /*index=5*/s32[96]{0:...) while((s32[]{:T(128)}, f32[8,128,256]{2,0,1:T(8,128)S(1)}, ...), condition=%wide.region_1.0_spmd.clone, body=%wide.region_0.0_spmd.clone.sunk | while | flops 143131984 | bytes 7870645 | solution.py:30
  154.1 0.7 compare_select_fusion.4
  154.9 2.8 gather_fusion
  157.7 1.5 fusion.59
  159.9 0.8 fusion.60
  160.7 0.7 compare_select_fusion.4
  161.5 2.8 gather_fusion
  164.3 1.5 fusion.59
  166.5 0.8 fusion.60
  168.0 2.8 gather_fusion
  170.8 1.5 fusion.59
  173.0 0.8 fusion.60
  174.6 2.8 gather_fusion
  177.4 1.5 fusion.59
  179.6 0.8 fusion.60
  181.2 2.8 gather_fusion
  184.0 1.5 fusion.59
  186.2 0.8 fusion.60
  187.7 2.8 gather_fusion
  190.5 1.5 fusion.59
  192.8 0.8 fusion.60
  193.6 1.3 copy.8
  195.0 40.6 %reduce-scatter.3.cloned.1.call-done = f32[128,256]{1,0:T(8,128)} async-done(((f32[1024,256]{1,0:T(8,128)}), f32[128,256]{1,0:T(8,128)}) %reduce-scatter.3.cloned.1.call-update) | async-done | bytes 131088 | tf_op jit(solution)/shard_map/reduce_scatter | solution.py:38
  235.6 1.7 fusion.33
  237.4 140.2 %all-gather.5.cloned.1.call-done = bf16[8192,256]{1,0:T(8,128)(2,1)} async-done(((bf16[128,256]{1,0:T(8,128)(2,1)}), bf16[8192,256]{1,0:T(8,128)(2,1)}) %all-gather.5.cloned.1.call-update) | async-done | bytes 4194320 | tf_op jit(solution)/shard_map/all_gather | solution.py:36
  377.6 35.3 %while.29 = (s32[]{:T(128)}, f32[8,128,256]{2,0,1:T(8,128)S(1)}, s32[96]{0:T(128)S(1)}, s32[]{:T(128)}, bf16[96,128,128]{2,1,0:T(8,128)(2,1)}, /*index=5*/s32[96...) while((s32[]{:T(128)}, f32[8,128,256]{2,0,1:T(8,128)S(1)}, ...), condition=%wide.region_4.5_spmd.clone, body=%wide.region_3.4_spmd.clone.sunk | while | flops 143131984 | bytes 7869081 | solution.py:30
  377.7 2.8 gather_fusion.1
  380.5 1.5 fusion.65
  382.7 0.8 fusion.66
  383.6 2.8 gather_fusion.1
  386.4 1.5 fusion.65
  388.6 0.8 fusion.66
  389.5 2.8 gather_fusion.1
  392.3 1.5 fusion.65
  394.5 0.8 fusion.66
  395.4 2.8 gather_fusion.1
  398.2 1.5 fusion.65
  400.4 0.8 fusion.66
  401.3 2.8 gather_fusion.1
  404.1 1.5 fusion.65
  406.3 0.8 fusion.66
  407.2 2.8 gather_fusion.1
  410.0 1.5 fusion.65
  412.2 0.8 fusion.66
  413.0 1.3 copy.9
  414.3 40.6 %reduce-scatter.5.cloned.1.call-done = f32[128,256]{1,0:T(8,128)} async-done(((f32[1024,256]{1,0:T(8,128)}), f32[128,256]{1,0:T(8,128)}) %reduce-scatter.5.cloned.1.call-update) | async-done | bytes 131088 | tf_op jit(solution)/shard_map/reduce_scatter | solution.py:38
  455.0 1.7 fusion.32
  (77 shorter events, 13.2 us)
Async XLA Ops:
  6.5 147.6 %all-gather.3.cloned.1.call-start = ((), (), s32[]{:S(2)}) async-start(), calls=%async_computation.2 | async-start | bytes 4259840 | tf_op jit(solution)/shard_map/all_gather | solution.py:36
  7.3 228.4 %reduce-scatter.3.cloned.1.call-start = ((), (), s32[]{:S(2)}) async-start(), calls=%async_computation.3 | async-start | bytes 1179648 | tf_op jit(solution)/shard_map/reduce_scatter | solution.py:38
  154.1 5.0 %copy-start.2 = (s32[96]{0:T(128)S(1)}, s32[96]{0:T(128)}, u32[]{:S(2)}) copy-start(s32[96]{0:T(128)} %get-tuple-element.477) | copy-start | bytes 1156 | tf_op jit(solution)/shard_map/while
  160.7 5.0 %copy-start.2 = (s32[96]{0:T(128)S(1)}, s32[96]{0:T(128)}, u32[]{:S(2)}) copy-start(s32[96]{0:T(128)} %get-tuple-element.477) | copy-start | bytes 1156 | tf_op jit(solution)/shard_map/while
  167.3 5.0 %copy-start.2 = (s32[96]{0:T(128)S(1)}, s32[96]{0:T(128)}, u32[]{:S(2)}) copy-start(s32[96]{0:T(128)} %get-tuple-element.477) | copy-start | bytes 1156 | tf_op jit(solution)/shard_map/while
  173.8 5.0 %copy-start.2 = (s32[96]{0:T(128)S(1)}, s32[96]{0:T(128)}, u32[]{:S(2)}) copy-start(s32[96]{0:T(128)} %get-tuple-element.477) | copy-start | bytes 1156 | tf_op jit(solution)/shard_map/while
  180.4 5.0 %copy-start.2 = (s32[96]{0:T(128)S(1)}, s32[96]{0:T(128)}, u32[]{:S(2)}) copy-start(s32[96]{0:T(128)} %get-tuple-element.477) | copy-start | bytes 1156 | tf_op jit(solution)/shard_map/while
  187.0 5.0 %copy-start.2 = (s32[96]{0:T(128)S(1)}, s32[96]{0:T(128)}, u32[]{:S(2)}) copy-start(s32[96]{0:T(128)} %get-tuple-element.477) | copy-start | bytes 1156 | tf_op jit(solution)/shard_map/while
  193.5 1.4 copy-start.1
  193.5 42.1 %copy-start = (bf16[2,256,256]{2,1,0:T(8,128)(2,1)S(1)}, bf16[2,256,256]{2,1,0:T(8,128)(2,1)}, u32[]{:S(2)}) copy-start(bf16[2,256,256]{2,1,0:T(8,128)(2,1)} %param.16) | copy-start | bytes 786436
  193.6 184.1 %copy-start.3 = (s32[96]{0:T(128)S(1)}, s32[96]{0:T(128)}, u32[]{:S(2)}) copy-start(s32[96]{0:T(128)} %get-tuple-element.536) | copy-start | bytes 1156
  193.6 184.1 %copy-start.4 = (s32[96]{0:T(128)S(1)}, s32[96]{0:T(128)}, u32[]{:S(2)}) copy-start(s32[96]{0:T(128)} %get-tuple-element.537) | copy-start | bytes 1156
  194.9 182.7 %all-gather.5.cloned.1.call-start = ((), (), s32[]{:S(2)}) async-start(), calls=%async_computation.4 | async-start | bytes 4259840 | tf_op jit(solution)/shard_map/all_gather | solution.py:36
  237.3 217.6 %reduce-scatter.5.cloned.1.call-start = ((), (), s32[]{:S(2)}) async-start(), calls=%async_computation.5 | async-start | bytes 1179648 | tf_op jit(solution)/shard_map/reduce_scatter | solution.py:38
Sparse Core Ops, SparseCore 0:
  10.3 143.7 all-gather.2
  195.0 40.5 reduce-scatter.2
  238.6 139.0 all-gather.4
  414.4 40.4 reduce-scatter.4
where the time goes:
time: 465 us; the launch traced here: 463 us
  waiting for transfers between devices  369 us (79%)
  local copies, waits for them, and re-layouts  37.2 us (8%)
  matrix products  30.1 us (6%)
  between operations  13.2 us (3%)
  other arithmetic  12.8 us (3%)
    all_gather x2, waiting for transfers between devices, one_layer(): gathered = lax.all_gather(hidden, 'rep', axis=0, tiled=True)  287 us
    reduce_scatter x2, waiting for transfers between devices, one_layer(): lax.psum_scatter(partial_value, 'loop', scatter_dimension=0, tiled=True)  81.3 us
    gather x12, local copies, waits for them, and re-layouts, accumulate(): src_rows = blocks[src_group]  33.6 us
    dot_general x12, matrix products, accumulate(): jnp.einsum('tab,tbf->taf', tile_group, src_rows, preferred_element_type=j...  17.6 us
  transfers between devices with their start and end apart: 4, of which 4 were waited for; matrix products, arithmetic and copies ran while one was open for 0% of the time, Pallas kernels for 0%

commit v1 on v0

v1 whole, which is shorter than its diff:
```python
import jax
import jax.numpy as jnp
from jax import lax
from jax.experimental import pallas as pl
from jax.experimental.pallas import tpu as pltpu
from jax.sharding import PartitionSpec as P

MESH = pl.DeviceIdType.MESH
NZ, NY, NL = 16, 4, 8
NREP = NZ * NY
B = 128
F = 256
SLOTS = 96
LAYERS = 2
CH = 2
FC = F // CH
RA = 48
RB = B - RA
PAIRS = (SLOTS + NL) // 2
PIECES_A = 2 * 8
NSEM = 96
LAG = 4


def order_tables(dst, src, count):
    n = SLOTS
    i32 = jnp.int32
    row = lax.broadcasted_iota(i32, (n, n), 0)
    col = lax.broadcasted_iota(i32, (n, n), 1)
    eye = row == col
    lane = lax.broadcasted_iota(i32, (1, n), 1)
    key_row = jnp.where(lane < count, dst, NL)
    key_col = jnp.sum(jnp.where(eye, key_row, 0), axis=1, keepdims=True)
    src_col = jnp.sum(jnp.where(eye, src, 0), axis=1, keepdims=True)
    rank = jnp.sum(jnp.where((key_col == key_row) & (col < row), 1, 0), axis=1, keepdims=True)
    lanes = lax.broadcasted_iota(i32, (n, B), 1)
    onehot = key_col == lanes
    number = jnp.sum(jnp.where(onehot, 1, 0), axis=0, keepdims=True)
    lane_b = lax.broadcasted_iota(i32, (1, B), 1)
    number = jnp.where(lane_b < NL, number, 0)
    pairs = (number + 1) // 2
    row_b = lax.broadcasted_iota(i32, (B, B), 0)
    col_b = lax.broadcasted_iota(i32, (B, B), 1)
    pairs_col = jnp.sum(jnp.where(row_b == col_b, pairs, 0), axis=1, keepdims=True)
    first = jnp.sum(jnp.where(row_b < col_b, pairs_col, 0), axis=0, keepdims=True)
    first_col = jnp.sum(jnp.where(row_b == col_b, first, 0), axis=1, keepdims=True)
    start = jnp.sum(jnp.where(onehot, first, 0), axis=1, keepdims=True)
    place = jnp.where(key_col < NL, 2 * start + rank, B)
    here = place == lanes
    slot_col = lax.broadcasted_iota(i32, (n, B), 0)
    slot = SLOTS + jnp.sum(jnp.where(here, slot_col - SLOTS, 0), axis=0, keepdims=True)
    source = jnp.sum(jnp.where(here, src_col, 0), axis=0, keepdims=True)
    opens = jnp.sum(jnp.where((first_col == col_b) & (pairs_col > 0), 1, 0), axis=0, keepdims=True)
    last = jnp.where(pairs > 0, first + pairs - 1, -1)
    return slot, source, 1 - opens, last


def kernel(
    features,
    tiles_hbm,
    dst_ref,
    src_ref,
    count_ref,
    weights,
    biases,
    out,
    h00,
    h01,
    h10,
    h11,
    tiles,
    table_v,
    table,
    runs0,
    runs1,
    outbox,
    inbox,
    own_sum,
    send_sems,
    recv_sems,
    local_sems,
):
    rep = lax.axis_index("rep")
    me = lax.axis_index("loop")
    z = rep // NY
    y = rep % NY
    held = ((h00, h01), (h10, h11))
    runs = (runs0, runs1)

    def zmod(v):
        return lax.rem(v + 2 * NZ, NZ)

    def ymod(v):
        return lax.rem(v + 2 * NY, NY)

    def at(zz, yy):
        return {"rep": zz * NY + yy}

    z_up, z_down = at(zmod(z + 1), y), at(zmod(z - 1), y)
    y_up, y_down, y_far = at(z, ymod(y + 1)), at(z, ymod(y - 1)), at(z, ymod(y + 2))
    mates = [{"loop": lax.rem(me + d, NL)} for d in range(1, NL)]

    barrier = pltpu.get_barrier_semaphore()
    everyone = [z_up, z_down, y_up, y_down, y_far] + mates
    for other in everyone:
        pl.semaphore_signal(barrier, inc=1, device_id=other, device_id_type=MESH)

    tiles_in = pltpu.make_async_copy(tiles_hbm, tiles.at[pl.ds(0, SLOTS)], local_sems.at[0])
    tiles_in.start()
    own_in = []
    for c in range(CH):
        copy = pltpu.make_async_copy(
            features.at[:, pl.ds(c * FC, FC)], held[0][c].at[rep], local_sems.at[1 + c]
        )
        copy.start()
        own_in.append(copy)
    pl.semaphore_wait(barrier, len(everyone))

    sent = []
    counter = [0]

    def fresh():
        counter[0] += 1
        return counter[0] - 1

    def send(ref, device, sem):
        copy = pltpu.make_async_remote_copy(
            src_ref=ref,
            dst_ref=ref,
            send_sem=send_sems.at[sem],
            recv_sem=recv_sems.at[sem],
            device_id=device,
            device_id_type=MESH,
        )
        copy.start()
        sent.append(copy)

    def landed(ref, sem):
        pltpu.make_async_remote_copy(
            src_ref=ref,
            dst_ref=ref,
            send_sem=send_sems.at[sem],
            recv_sem=recv_sems.at[sem],
            device_id=z_up,
            device_id_type=MESH,
        ).wait_recv()

    def drain():
        for copy in sent:
            copy.wait_send()
        sent.clear()

    half = NZ // 2

    def gather(k, c):
        h = held[k][c]
        sems = {}

        def sem(*name):
            if name not in sems:
                sems[name] = fresh()
            return sems[name]

        def part_a(off, far=0):
            base = pl.multiple_of(zmod(z + off) * NY, NY)
            if far == 0:
                return h.at[pl.ds(base, NY), pl.ds(0, RA), :]
            return h.at[pl.ds(base + (NY // 2) * (far - 1), NY // 2), pl.ds(0, RA), :]

        def part_b(off, dy=0, far=0):
            block = zmod(z + off) * NY + ymod(y + dy)
            cut = 48 if c == 0 else 32
            if far == 0:
                return h.at[block, pl.ds(RA, RB), :]
            if far == 1:
                return h.at[block, pl.ds(RA, cut), :]
            return h.at[block, pl.ds(RA + cut, RB - cut), :]

        def z_send(part, name, i):
            up = half if i == half else 0
            send(part(-(i - 1), far=1 if up else 0), z_up, sem(name, "up", i))
            send(part(i - 1, far=2 if up else 0), z_down, sem(name, "down", i))

        def z_landed(part, name, i):
            far = i == half
            landed(part(-i, far=1 if far else 0), sem(name, "up", i))
            landed(part(i, far=2 if far else 0), sem(name, "down", i))

        def y_send(off):
            send(part_b(off), y_up, sem("yb", "up", off))
            send(part_b(off), y_down, sem("yb", "down", off))

        def y_relay(off):
            landed(part_b(off, -1), sem("yb", "up", off))
            landed(part_b(off, 1), sem("yb", "down", off))
            if off % 2 == 0:
                send(part_b(off, -1), y_up, sem("yb", "far", off))
            else:
                send(part_b(off, 1), y_down, sem("yb", "far", off))

        def y_end(off):
            landed(part_b(off, 2), sem("yb", "far", off))

        def offs(i):
            if i < 0:
                return ()
            return (0,) if i == 0 else ((half,) if i == half else (-i, i))

        z_send(part_b, "zb", 1)
        own_a = h.at[rep, pl.ds(0, RA), :]
        send(own_a, y_up, sem("ya", 1))
        send(own_a, y_down, sem("ya", 3))
        send(own_a, y_far, sem("ya", 2))
        y_send(0)
        yield
        for d in (1, 3, 2):
            landed(h.at[z * NY + ymod(y - d), pl.ds(0, RA), :], sem("ya", d))
        z_send(part_a, "za", 1)
        yield
        for i in range(1, half + 3):
            if i <= half:
                z_landed(part_b, "zb", i)
                if i < half:
                    z_send(part_b, "zb", i + 1)
                for off in offs(i):
                    y_send(off)
                z_landed(part_a, "za", i)
                if i < half:
                    z_send(part_a, "za", i + 1)
            if i - 1 <= half:
                for off in offs(i - 1):
                    y_relay(off)
            for off in offs(i - 2):
                y_end(off)
            yield

    def multiply(k, c, first, count):
        h, total = held[k][c], runs[c]

        def pair(p):
            a, b = 2 * p, 2 * p + 1
            left = jnp.concatenate([tiles[table[0, a]], tiles[table[0, b]]], axis=1)
            right = jnp.concatenate([h[table[1, a]], h[table[1, b]]], axis=0)
            return jnp.dot(left, right, preferred_element_type=jnp.float32)

        def step(i, unused):
            p = first + 2 * i
            one, two = pair(p), pair(p + 1)
            one = jnp.where(table[2, p] > 0, total[p], 0.0) + one
            total[p + 1] = one
            total[p + 2] = jnp.where(table[2, p + 1] > 0, one, 0.0) + two
            return unused

        lax.fori_loop(0, count // 2, step, 0)

    def box(k, c, d):
        return ((k * CH + c) * NL + d)

    def destination(c, d):
        j = lax.rem(me + d, NL)
        end = table[3, j]
        return jnp.where(end >= 0, runs[c][jnp.maximum(end, 0) + 1], 0.0)

    def scatter(k, c):
        base = [fresh() for _ in range(NL - 1)]
        for d in (4, 3, 5, 2, 6, 1, 7):
            outbox[box(k, c, d)] = destination(c, d).astype(jnp.bfloat16)
            copy = pltpu.make_async_remote_copy(
                src_ref=outbox.at[box(k, c, d)],
                dst_ref=inbox.at[box(k, c, d)],
                send_sem=send_sems.at[base[d - 1]],
                recv_sem=recv_sems.at[base[d - 1]],
                device_id=mates[d - 1],
                device_id_type=MESH,
            )
            copy.start()
            sent.append(copy)
        own_sum[c] = destination(c, 0)
        return base

    def collect(k, c, base):
        total = own_sum[c]
        for d in (1, 7, 2, 6, 3, 5, 4):
            landed(inbox.at[box(k, c, d)], base[d - 1])
            total = total + inbox[box(k, c, d)].astype(jnp.float32)
        return jnp.dot(
            total.astype(jnp.bfloat16),
            weights[k, pl.ds(c * FC, FC), :],
            preferred_element_type=jnp.float32,
        )

    def tables():
        tiles[SLOTS] = jnp.zeros((B, B), jnp.bfloat16)
        for c in range(CH):
            runs[c][0] = jnp.zeros((B, FC), jnp.float32)
        for i, row in enumerate(order_tables(dst_ref[...], src_ref[...], count_ref[0])):
            table_v[pl.ds(i, 1), :] = row
        copy = pltpu.make_async_copy(table_v, table, local_sems.at[3])
        copy.start()
        return copy

    table_in = None
    for k in range(LAYERS):
        first, second = gather(k, 0), gather(k, 1)
        if k == 0:
            own_in[0].wait()
        next(first)
        if k == 0:
            own_in[1].wait()
            table_in = tables()
        for _ in range(LAG):
            next(first)
        live = True
        while True:
            try:
                next(first)
            except StopIteration:
                break
            next(second)
        if k == 0:
            tiles_in.wait()
            table_in.wait()
        share = 2 * -(-PAIRS // (2 * LAG))
        done = 0
        for _ in second:
            take = min(share, PAIRS - done)
            if take > 0:
                multiply(k, 0, done, take)
                done += take
        if done < PAIRS:
            multiply(k, 0, done, PAIRS - done)
        base0 = scatter(k, 0)
        multiply(k, 1, 0, PAIRS)
        base1 = scatter(k, 1)
        mixed = collect(k, 0, base0)
        drain()
        mixed = mixed + collect(k, 1, base1) + biases[pl.ds(k, 1), :]
        hidden = jnp.maximum(mixed, 0.0).astype(jnp.bfloat16)
        if k + 1 < LAYERS:
            for c in range(CH):
                held[k + 1][c][rep] = hidden[:, c * FC : (c + 1) * FC]
        else:
            out[...] = hidden
    drain()


def body(features, tiles, tile_dst, tile_src, tile_count, weights, biases):
    vmem, anyspace = pl.BlockSpec(memory_space=pltpu.VMEM), pl.BlockSpec(memory_space=pl.ANY)
    smem = pl.BlockSpec(memory_space=pltpu.SMEM)
    block = pltpu.VMEM((NREP, B, FC), jnp.bfloat16)
    return pl.pallas_call(
        kernel,
        out_shape=jax.ShapeDtypeStruct((B, F), jnp.bfloat16),
        in_specs=[anyspace, anyspace, vmem, vmem, smem, vmem, vmem],
        out_specs=vmem,
        scratch_shapes=[
            block,
            block,
            block,
            block,
            pltpu.VMEM((SLOTS + 1, B, B), jnp.bfloat16),
            pltpu.VMEM((8, B), jnp.int32),
            pltpu.SMEM((8, B), jnp.int32),
            pltpu.VMEM((PAIRS + 1, B, FC), jnp.float32),
            pltpu.VMEM((PAIRS + 1, B, FC), jnp.float32),
            pltpu.VMEM((LAYERS * CH * NL, B, FC), jnp.bfloat16),
            pltpu.VMEM((LAYERS * CH * NL, B, FC), jnp.bfloat16),
            pltpu.VMEM((CH, B, FC), jnp.float32),
            pltpu.SemaphoreType.DMA((LAYERS * CH * NSEM,)),
            pltpu.SemaphoreType.DMA((LAYERS * CH * NSEM,)),
            pltpu.SemaphoreType.DMA((4,)),
        ],
        compiler_params=pltpu.CompilerParams(
            collective_id=0, has_side_effects=True, vmem_limit_bytes=48 * 1024 * 1024
        ),
        cost_estimate=pl.CostEstimate(flops=2 * LAYERS * SLOTS * B * B * F, bytes_accessed=4 << 20, transcendentals=0),
    )(
        features,
        tiles,
        tile_dst.reshape(1, SLOTS),
        tile_src.reshape(1, SLOTS),
        tile_count,
        weights,
        biases,
    )


def solution(mesh):
    in_specs = (
        P(("rep", "loop"), None),
        P(("rep", "loop"), None, None),
        P(("rep", "loop")),
        P(("rep", "loop")),
        P(("rep", "loop")),
        P(),
        P(),
    )
    out_specs = P(("rep", "loop"), None)
    return jax.shard_map(body, mesh=mesh, in_specs=in_specs, out_specs=out_specs, check_vma=False)
```

time: 465 us -> 163 us (0.35)
  waiting for transfers between devices: 369 us -> 0 us
  Pallas kernels: 0 us -> 156 us
  local copies, waits for them, and re-layouts: 37.2 us -> 6.29 us
  matrix products: 30.1 us -> 0 us
  other arithmetic: 12.8 us -> 0 us
  between operations: 13.2 us -> 0.67 us
    all_gather x2 -> x0, waiting for transfers between devices: 287 us -> none  [one_layer(): gathered = lax.all_gather(hidden, 'rep', axis=0, tiled=True)]
    pallas_call x0 -> x1, Pallas kernels: none -> 156 us  [body(): pl.pallas_call(kernel, out_shape=jax.ShapeDtypeStruct((B, F), jnp.bfloat1...]
    reduce_scatter x2 -> x0, waiting for transfers between devices: 81.3 us -> none  [one_layer(): lax.psum_scatter(partial_value, 'loop', scatter_dimension=0, tiled=True)]
    gather x12 -> x0, local copies, waits for them, and re-layouts: 33.6 us -> none  [accumulate(): src_rows = blocks[src_group]]
    dot_general x26 -> x0, matrix products: 30.1 us -> none  [the longest x12 17.6 us: accumulate(): jnp.einsum('tab,tbf->taf', tile_group, src_rows, preferred_element_type=j...]
    lt x12 -> x0, other arithmetic: 7.81 us -> none  [accumulate(): valid = start + jnp.arange(group, dtype=jnp.int32) < occupied]
    unnamed x8 -> x13, local copies, waits for them, and re-layouts: 0.03 us -> 6.29 us
    select_n x12 -> x0, other arithmetic: 4.89 us -> none  [accumulate(): src_rows = blocks[src_group]]
  transfers between devices with their start and end apart: 4 -> 0, of which waited for: 4 -> 0; matrix products, arithmetic and copies ran while one was open for 0% -> 0% of each run, Pallas kernels for 0% -> 0%
where the time goes in v1:
time: 163 us
  Pallas kernels  156 us (96%)
  local copies, waits for them, and re-layouts  6.29 us (4%)
    pallas_call x1, Pallas kernels, body(): pl.pallas_call(kernel, out_shape=jax.ShapeDtypeStruct((B, F), jnp.bfloat1...  156 us
    unnamed x13, local copies, waits for them, and re-layouts  6.29 us

profile of v1, /device:TPU:1, one launch (start us, length us, event | category | flops | bytes accessed | tf_op | source)
XLA Modules:
  0.0 162.9 jit_solution(7305521763163397466)
XLA Ops:
  0.7 0.0 copy-start
  0.7 1.9 %copy-done = bf16[96,128,128]{2,1,0:T(8,128)(2,1)S(1)} copy-done((bf16[96,128,128]{2,1,0:T(8,128)(2,1)S(1)}, bf16[96,128,128]{2,1,0:T(8,128)(2,1)}, u32[]{:S(2)}) %copy-start) | copy-done | bytes 3145752
  2.5 0.0 copy-start.1
  2.5 0.9 copy-done.1
  3.5 0.0 copy-start.2
  3.5 0.8 copy-done.2
  4.3 0.0 copy-start.3
  4.3 0.7 copy-done.3
  5.0 0.0 copy-start.4
  5.0 0.7 copy-done.4
  5.7 0.0 copy-start.5
  5.7 0.7 copy-done.5
  6.3 155.9 %shard_map.73 = bf16[128,256]{1,0:T(8,128)(2,1)S(1)} custom-call(bf16[128,256]{1,0:T(8,128)(2,1)S(1)} %copy-done.2, bf16[96,128,128]{2,1,0:T(8,128)(2,1)S(1)} %copy-done, s32[1,96]{1,0:T(1,128)S(1)} %bitcast.2, s32[1,96]{1,0:T(1,128)S(1)} %bitcast.3, s32[1]{0:T(128)S(6)} %copy.9.count_ref, bf16[2,256,256]{2,1,0:T(8,128)(2,1)S(1)} %copy-done.1, ...), custom_call_target="tpu_custom_call" | custom-call | flops 1610612736 | bytes 4194304 | tf_op jit(solution)/shard_map/pallas_call | solution.py:351
  162.2 0.6 copy.10
Async XLA Ops:
  0.7 1.9 %copy-start = (bf16[96,128,128]{2,1,0:T(8,128)(2,1)S(1)}, bf16[96,128,128]{2,1,0:T(8,128)(2,1)}, u32[]{:S(2)}) copy-start(bf16[96,128,128]{2,1,0:T(8,128)(2,1)} %tiles_hbm.1) | copy-start | bytes 9437188
  2.5 0.9 copy-start.1
  3.5 0.8 copy-start.2
  4.3 0.7 copy-start.3
  5.0 0.7 copy-start.4
  5.7 0.7 copy-start.5

commit v2 on v0

v2 whole, which is shorter than its diff:
```python
import jax
import jax.numpy as jnp
from jax import lax
from jax.experimental import pallas as pl
from jax.experimental.pallas import tpu as pltpu
from jax.sharding import PartitionSpec as P

MESH = pl.DeviceIdType.MESH
NZ, NY, NL = 16, 4, 8
NREP = NZ * NY
B = 128
F = 256
SLOTS = 96
LAYERS = 2
RA = 48
RB = B - RA
CUT = 48
VMEM = 62 * 1024 * 1024
HALF = NZ // 2
PAIRS = (SLOTS + NL) // 2
ZB, ZA = 0, 2 * (HALF + 1)
YA = ZA + NY * 2 * (HALF + 1)
YB = YA + NY
RS = YB + 3 * NZ
NSEM = RS + NL


def order_tables(dst, src, count):
    n = SLOTS
    i32 = jnp.int32
    row = lax.broadcasted_iota(i32, (n, n), 0)
    col = lax.broadcasted_iota(i32, (n, n), 1)
    eye = row == col
    lane = lax.broadcasted_iota(i32, (1, n), 1)
    key_row = jnp.where(lane < count, dst, NL)
    key_col = jnp.sum(jnp.where(eye, key_row, 0), axis=1, keepdims=True)
    src_col = jnp.sum(jnp.where(eye, src, 0), axis=1, keepdims=True)
    rank = jnp.sum(jnp.where((key_col == key_row) & (col < row), 1, 0), axis=1, keepdims=True)
    lanes = lax.broadcasted_iota(i32, (n, B), 1)
    onehot = key_col == lanes
    number = jnp.sum(jnp.where(onehot, 1, 0), axis=0, keepdims=True)
    lane_b = lax.broadcasted_iota(i32, (1, B), 1)
    number = jnp.where(lane_b < NL, number, 0)
    pairs = (number + 1) // 2
    row_b = lax.broadcasted_iota(i32, (B, B), 0)
    col_b = lax.broadcasted_iota(i32, (B, B), 1)
    pairs_col = jnp.sum(jnp.where(row_b == col_b, pairs, 0), axis=1, keepdims=True)
    first = jnp.sum(jnp.where(row_b < col_b, pairs_col, 0), axis=0, keepdims=True)
    first_col = jnp.sum(jnp.where(row_b == col_b, first, 0), axis=1, keepdims=True)
    start = jnp.sum(jnp.where(onehot, first, 0), axis=1, keepdims=True)
    place = jnp.where(key_col < NL, 2 * start + rank, B)
    here = place == lanes
    slot_col = lax.broadcasted_iota(i32, (n, B), 0)
    slot = SLOTS + jnp.sum(jnp.where(here, slot_col - SLOTS, 0), axis=0, keepdims=True)
    source = jnp.sum(jnp.where(here, src_col, 0), axis=0, keepdims=True)
    opens = jnp.sum(jnp.where((first_col == col_b) & (pairs_col > 0), 1, 0), axis=0, keepdims=True)
    last = jnp.where(pairs > 0, first + pairs - 1, -1)
    return slot, source, 1 - opens, last


def kernel(
    features,
    tiles_hbm,
    dst_hbm,
    src_hbm,
    count_ref,
    weights_hbm,
    biases_hbm,
    out,
    h0,
    h1,
    tiles,
    dst_ref,
    src_ref,
    weights,
    biases,
    table_v,
    table,
    runs,
    outbox,
    inbox,
    send_sems,
    recv_sems,
    local_sems,
):
    rep = lax.axis_index("rep")
    me = lax.axis_index("loop")
    z = rep // NY
    y = rep % NY
    held = (h0, h1)

    def zmod(v):
        return lax.rem(v + 2 * NZ, NZ)

    def ymod(v):
        return lax.rem(v + 2 * NY, NY)

    def at(zz, yy):
        return {"rep": zz * NY + yy}

    z_up, z_down = at(zmod(z + 1), y), at(zmod(z - 1), y)
    y_up, y_down, y_far = at(z, ymod(y + 1)), at(z, ymod(y - 1)), at(z, ymod(y + 2))
    mates = [{"loop": lax.rem(me + d, NL)} for d in range(1, NL)]

    barrier = pltpu.get_barrier_semaphore()
    everyone = [z_up, z_down, y_up, y_down, y_far] + mates
    for other in everyone:
        pl.semaphore_signal(barrier, inc=1, device_id=other, device_id_type=MESH)

    copies = [
        pltpu.make_async_copy(a, b, local_sems.at[i])
        for i, (a, b) in enumerate(
            (
                (features, h0.at[rep]),
                (dst_hbm, dst_ref),
                (src_hbm, src_ref),
                (tiles_hbm, tiles.at[pl.ds(0, SLOTS)]),
                (weights_hbm, weights),
                (biases_hbm, biases),
            )
        )
    ]
    for copy in copies:
        copy.start()
    own_in, dst_in, src_in, *later_in = copies
    table_in = pltpu.make_async_copy(table_v, table, local_sems.at[len(copies)])
    pl.semaphore_wait(barrier, len(everyone))

    def tables():
        tiles[SLOTS] = jnp.zeros((B, B), jnp.bfloat16)
        runs[0] = jnp.zeros((B, F), jnp.float32)
        dst_in.wait()
        src_in.wait()
        table_v[...] = jnp.zeros_like(table_v)
        for i, row in enumerate(order_tables(dst_ref[...], src_ref[...], count_ref[0])):
            table_v[pl.ds(i, 1), :] = row
        table_in.start()

    def gather(k, meanwhile):
        h = held[k]

        def link(src, dst, sem, device):
            return pltpu.make_async_remote_copy(
                src_ref=src,
                dst_ref=dst,
                send_sem=send_sems.at[k * NSEM + sem],
                recv_sem=recv_sems.at[k * NSEM + sem],
                device_id=device,
                device_id_type=MESH,
            )

        def send(ref, sem, device):
            link(ref, ref, sem, device).start()

        def landed(ref, sem):
            link(ref, ref, sem, z_up).wait_recv()

        def gone(ref, sem):
            link(ref, ref, sem, z_up).wait_send()

        def block(off, dy):
            return zmod(z + off) * NY + ymod(y + dy)

        def rows_a(off, dy):
            return h.at[block(off, dy), pl.ds(0, RA), :]

        def rows_b(off, dy=0, up=None):
            if up is None:
                return h.at[block(off, dy), pl.ds(RA, RB), :]
            return h.at[block(off, dy), pl.ds(RA, CUT) if up else pl.ds(RA + CUT, RB - CUT), :]

        def sem_zb(up, i):
            return ZB + (0 if up else HALF + 1) + i

        def sem_za(dy, up, i):
            return ZA + (2 * dy + (0 if up else 1)) * (HALF + 1) + i

        def sem_yb(way, off):
            return YB + way * NZ + zmod(off)

        def hop_b(do, i, last=False):
            for up in (True, False):
                off = -i if up else i
                do(rows_b(off, up=up if last else None), sem_zb(up, i), up)

        def hop_a(do, dy, i, last=False):
            for up in (True, False):
                if not last or up == (dy < 2):
                    do(rows_a(-i if up else i, dy), sem_za(dy, up, i), up)

        def forward(ref_of, dy, i, last):
            def do(unused, sem, up):
                off = -(i - 1) if up else i - 1
                if dy is None:
                    ref = rows_b(off, up=up if last else None)
                else:
                    ref = rows_a(off, dy)
                send(ref, sem, z_up if up else z_down)

            return do

        def send_b(i, last=False):
            hop_b(forward(rows_b, None, i, last), i, last)

        def send_a(dy, i, last=False):
            hop_a(forward(rows_a, dy, i, last), dy, i, last)

        def wait(ref, sem, up):
            landed(ref, sem)

        def y_send(off):
            send(rows_b(off), sem_yb(0, off), y_up)
            send(rows_b(off), sem_yb(1, off), y_down)

        def y_relay(off, parity):
            landed(rows_b(off, -1), sem_yb(0, off))
            landed(rows_b(off, 1), sem_yb(1, off))
            way = 1 - 2 * parity
            send(rows_b(off, -way), sem_yb(2, off), at(z, ymod(y + way)))

        def y_end(off):
            landed(rows_b(off, 2), sem_yb(2, off))

        others = (3, 1, 2)
        own_a = rows_a(0, 0)
        send_b(1)
        send_a(0, 1)
        for dy, device in ((1, y_up), (3, y_down), (2, y_far)):
            send(own_a, YA + dy, device)
        y_send(0)
        meanwhile()
        hop_b(wait, 1)
        send_b(2)
        y_send(-1)
        y_send(1)
        hop_a(wait, 0, 1)
        send_a(0, 2)
        for dy in others:
            landed(rows_a(0, dy), YA + NY - dy)
            send_a(dy, 1)
        y_relay(0, 0)

        def middle(i, unused):
            hop_b(wait, i)
            send_b(i + 1)
            y_send(-i)
            y_send(i)
            hop_a(wait, 0, i)
            send_a(0, i + 1)
            for dy in others:
                hop_a(wait, dy, i - 1)
                send_a(dy, i)
            y_relay(-(i - 1), lax.rem(i - 1, 2))
            y_relay(i - 1, lax.rem(i - 1, 2))
            return unused

        lax.fori_loop(2, HALF - 1, middle, 0)
        i = HALF - 1
        hop_b(wait, i)
        send_b(HALF, True)
        y_send(-i)
        y_send(i)
        hop_a(wait, 0, i)
        send_a(0, HALF, True)
        for dy in others:
            hop_a(wait, dy, i - 1)
            send_a(dy, i)
        y_relay(-(i - 1), (i - 1) % 2)
        y_relay(i - 1, (i - 1) % 2)
        i = HALF
        hop_b(wait, i, True)
        y_send(i)
        for dy in others:
            hop_a(wait, dy, i - 1)
            send_a(dy, i, True)
        y_relay(-(i - 1), (i - 1) % 2)
        y_relay(i - 1, (i - 1) % 2)
        hop_a(wait, 0, i, True)
        y_relay(i, i % 2)
        for dy in others:
            hop_a(wait, dy, i, True)

        def arrive(off, unused):
            y_end(off)
            return unused

        lax.fori_loop(0, NZ, arrive, 0)

        def drain():
            def sent(ref, sem, up):
                gone(ref, sem)

            def hops(i, unused):
                hop_b(sent, i)
                for dy in range(NY):
                    hop_a(sent, dy, i)
                return unused

            lax.fori_loop(1, HALF, hops, 0)
            hop_b(sent, HALF, True)
            for dy in range(NY):
                hop_a(sent, dy, HALF, True)
            for dy in others:
                gone(own_a, YA + dy)

            def ways(j, unused):
                gone(rows_b(0), YB + j)
                return unused

            lax.fori_loop(0, 3 * NZ, ways, 0)

        return drain

    def multiply(k):
        h = held[k]

        def pair(p):
            a, b = 2 * p, 2 * p + 1
            left = jnp.concatenate([tiles[table[0, a]], tiles[table[0, b]]], axis=1)
            right = jnp.concatenate([h[table[1, a]], h[table[1, b]]], axis=0)
            return jnp.dot(left, right, preferred_element_type=jnp.float32)

        def step(i, unused):
            for p in (2 * i, 2 * i + 1):
                runs[p + 1] = jnp.where(table[2, p] > 0, runs[p], 0.0) + pair(p)
            return unused

        lax.fori_loop(0, PAIRS // 2, step, 0)

    def destination(d):
        end = table[3, lax.rem(me + d, NL)]
        return jnp.where(end >= 0, runs[jnp.maximum(end, 0) + 1], 0.0)

    def partial_copy(k, d):
        return pltpu.make_async_remote_copy(
            src_ref=outbox.at[k * NL + d],
            dst_ref=inbox.at[k * NL + d],
            send_sem=send_sems.at[k * NSEM + RS + d],
            recv_sem=recv_sems.at[k * NSEM + RS + d],
            device_id=mates[d - 1],
            device_id_type=MESH,
        )

    def reduce(k, meanwhile):
        for d in (4, 3, 5, 2, 6, 1, 7):
            outbox[k * NL + d] = destination(d).astype(jnp.bfloat16)
            partial_copy(k, d).start()
        meanwhile()
        total = destination(0)
        for d in (1, 7, 2, 6, 3, 5, 4):
            partial_copy(k, d).wait_recv()
            total = total + inbox[k * NL + d].astype(jnp.float32)
        return total.astype(jnp.bfloat16)

    own_in.wait()
    drain = None
    for k in range(LAYERS):
        drain = gather(k, tables if k == 0 else drain)
        if k == 0:
            table_in.wait()
            for copy in later_in:
                copy.wait()
        multiply(k)
        aggregate = reduce(k, drain if k + 1 == LAYERS else lambda: None)
        mixed = jnp.dot(aggregate, weights[k], preferred_element_type=jnp.float32) + biases[pl.ds(k, 1), :]
        hidden = jnp.maximum(mixed, 0.0).astype(jnp.bfloat16)
        if k + 1 < LAYERS:
            held[k + 1][rep] = hidden
        else:
            out[...] = hidden
    for i in range(LAYERS):
        for d in range(1, NL):
            partial_copy(i, d).wait_send()


def body(features, tiles, tile_dst, tile_src, tile_count, weights, biases):
    vmem, anyspace = pl.BlockSpec(memory_space=pltpu.VMEM), pl.BlockSpec(memory_space=pl.ANY)
    smem = pl.BlockSpec(memory_space=pltpu.SMEM)
    block = pltpu.VMEM((NREP, B, F), jnp.bfloat16)
    return pl.pallas_call(
        kernel,
        out_shape=jax.ShapeDtypeStruct((B, F), jnp.bfloat16),
        in_specs=[anyspace, anyspace, anyspace, anyspace, smem, anyspace, anyspace],
        out_specs=vmem,
        scratch_shapes=[
            block,
            block,
            pltpu.VMEM((SLOTS + 1, B, B), jnp.bfloat16),
            pltpu.VMEM((1, SLOTS), jnp.int32),
            pltpu.VMEM((1, SLOTS), jnp.int32),
            pltpu.VMEM((LAYERS, F, F), jnp.bfloat16),
            pltpu.VMEM((LAYERS, F), jnp.float32),
            pltpu.VMEM((8, B), jnp.int32),
            pltpu.SMEM((8, B), jnp.int32),
            pltpu.VMEM((PAIRS + 1, B, F), jnp.float32),
            pltpu.VMEM((LAYERS * NL, B, F), jnp.bfloat16),
            pltpu.VMEM((LAYERS * NL, B, F), jnp.bfloat16),
            pltpu.SemaphoreType.DMA((LAYERS * NSEM,)),
            pltpu.SemaphoreType.DMA((LAYERS * NSEM,)),
            pltpu.SemaphoreType.DMA((8,)),
        ],
        compiler_params=pltpu.CompilerParams(
            collective_id=0, has_side_effects=True, vmem_limit_bytes=VMEM
        ),
        cost_estimate=pl.CostEstimate(flops=2 * LAYERS * SLOTS * B * B * F, bytes_accessed=4 << 20, transcendentals=0),
    )(
        features,
        tiles,
        tile_dst.reshape(1, SLOTS),
        tile_src.reshape(1, SLOTS),
        tile_count,
        weights,
        biases,
    )


def solution(mesh):
    in_specs = (
        P(("rep", "loop"), None),
        P(("rep", "loop"), None, None),
        P(("rep", "loop")),
        P(("rep", "loop")),
        P(("rep", "loop")),
        P(),
        P(),
    )
    out_specs = P(("rep", "loop"), None)
    return jax.shard_map(body, mesh=mesh, in_specs=in_specs, out_specs=out_specs, check_vma=False)
```

time: 465 us -> 117 us (0.25)
  waiting for transfers between devices: 369 us -> 0 us
  Pallas kernels: 0 us -> 115 us
  local copies, waits for them, and re-layouts: 37.2 us -> 1.47 us
  matrix products: 30.1 us -> 0 us
  other arithmetic: 12.8 us -> 0 us
  between operations: 13.2 us -> 0.66 us
    all_gather x2 -> x0, waiting for transfers between devices: 287 us -> none  [one_layer(): gathered = lax.all_gather(hidden, 'rep', axis=0, tiled=True)]
    pallas_call x0 -> x1, Pallas kernels: none -> 115 us  [body(): pl.pallas_call(kernel, out_shape=jax.ShapeDtypeStruct((B, F), jnp.bfloat1...]
    reduce_scatter x2 -> x0, waiting for transfers between devices: 81.3 us -> none  [one_layer(): lax.psum_scatter(partial_value, 'loop', scatter_dimension=0, tiled=True)]
    gather x12 -> x0, local copies, waits for them, and re-layouts: 33.6 us -> none  [accumulate(): src_rows = blocks[src_group]]
    dot_general x26 -> x0, matrix products: 30.1 us -> none  [the longest x12 17.6 us: accumulate(): jnp.einsum('tab,tbf->taf', tile_group, src_rows, preferred_element_type=j...]
    lt x12 -> x0, other arithmetic: 7.81 us -> none  [accumulate(): valid = start + jnp.arange(group, dtype=jnp.int32) < occupied]
    select_n x12 -> x0, other arithmetic: 4.89 us -> none  [accumulate(): src_rows = blocks[src_group]]
  transfers between devices with their start and end apart: 4 -> 0, of which waited for: 4 -> 0; matrix products, arithmetic and copies ran while one was open for 0% -> 0% of each run, Pallas kernels for 0% -> 0%
where the time goes in v2:
time: 117 us
  Pallas kernels  115 us (98%)
  local copies, waits for them, and re-layouts  1.47 us (1%)
    pallas_call x1, Pallas kernels, body(): pl.pallas_call(kernel, out_shape=jax.ShapeDtypeStruct((B, F), jnp.bfloat1...  115 us

profile of v2, /device:TPU:1, one launch (start us, length us, event | category | flops | bytes accessed | tf_op | source)
XLA Modules:
  0.0 116.7 jit_solution(18016413372625406146)
XLA Ops:
  0.7 114.5 %shard_map.73 = bf16[128,256]{1,0:T(8,128)(2,1)} custom-call(bf16[128,256]{1,0:T(8,128)(2,1)} %features.1, bf16[96,128,128]{2,1,0:T(8,128)(2,1)} %tiles_hbm.1, s32[1,96]{1,0:T(1,128)} %bitcast.2, s32[1,96]{1,0:T(1,128)} %bitcast.3, s32[1]{0:T(128)S(6)} %copy.9.count_ref, bf16[2,256,256]{2,1,0:T(8,128)(2,1)} %weights_hbm.1, f32[2,256]{1,0:T(2,128)} %biases_hbm.1), custom_call_target="tpu_custom_call" | custom-call | flops 1610612736 | bytes 4194304 | tf_op jit(solution)/shard_map/pallas_call | solution.py:380
  115.2 1.5 %copy.10 = bf16[128,256]{1,0:T(8,128)(2,1)} copy(bf16[128,256]{1,0:T(8,128)(2,1)} %shard_map.73) | data formatting | bytes 131072

commit v3 on v0

v3 whole, which is shorter than its diff:
```python
import jax
import jax.numpy as jnp
from jax import lax
from jax.experimental import pallas as pl
from jax.experimental.pallas import tpu as pltpu
from jax.sharding import PartitionSpec as P

MESH = pl.DeviceIdType.MESH
NZ, NY, NL = 16, 4, 8
NREP = NZ * NY
B = 128
F = 256
SLOTS = 96
LAYERS = 2
RA = 48
RB = B - RA
CUT = 48
VMEM = 62 * 1024 * 1024
HALF = NZ // 2
CELLS = NL * NREP
ZB, ZA = 0, 2 * (HALF + 1)
YA = ZA + NY * 2 * (HALF + 1)
YB = YA + NY
RS = YB + 3 * NZ
NSEM = RS + NL
ORDER = (
    ("zb", 0, 1), ("zb", 1, 1), ("za", 0, 0, 1), ("ya", 3), ("ya", 1), ("za", 0, 1, 1), ("zb", 0, 2), ("zb", 1, 2),
    ("yo", 0), ("za", 3, 0, 1), ("ya", 2), ("yr", 15), ("za", 3, 1, 1), ("za", 1, 1, 1), ("za", 1, 0, 1), ("yr", 0),
    ("za", 0, 0, 2), ("za", 0, 1, 2), ("zb", 1, 3), ("zb", 0, 3), ("za", 2, 0, 1), ("za", 3, 1, 2), ("za", 3, 0, 2),
    ("yo", 14), ("yr", 1), ("za", 2, 1, 1), ("za", 1, 0, 2), ("yo", 2), ("za", 1, 1, 2), ("yo", 15), ("yr", 2),
    ("za", 0, 0, 3), ("za", 0, 1, 3), ("yr", 14), ("yr", 13), ("zb", 0, 4), ("zb", 1, 4), ("za", 2, 1, 2),
    ("za", 3, 0, 3), ("za", 3, 1, 3), ("za", 1, 0, 3), ("za", 1, 1, 3), ("ye", 15), ("za", 2, 0, 2), ("yr", 3),
    ("g", 15), ("za", 0, 0, 4), ("ye", 0), ("za", 0, 1, 4), ("ye", 1), ("yo", 1), ("yo", 13), ("zb", 0, 5),
    ("zb", 1, 5), ("za", 3, 1, 4), ("za", 3, 0, 4), ("ye", 2), ("g", 0), ("za", 2, 0, 3), ("za", 1, 0, 4),
    ("za", 1, 1, 4), ("g", 1), ("ye", 13), ("za", 2, 1, 3), ("za", 0, 0, 5), ("yr", 12), ("ye", 14), ("yr", 4),
    ("za", 0, 1, 5), ("zb", 0, 6), ("zb", 1, 6), ("g", 14), ("yo", 5), ("yo", 3), ("za", 1, 0, 5), ("za", 3, 1, 5),
    ("yo", 4), ("za", 3, 0, 5), ("za", 2, 0, 4), ("ye", 3), ("za", 2, 1, 4), ("za", 1, 1, 5), ("yr", 5),
    ("za", 0, 0, 6), ("g", 13), ("ye", 12), ("zb", 1, 7), ("za", 0, 1, 6), ("g", 3), ("zb", 0, 7), ("za", 3, 0, 6),
    ("g", 2), ("za", 2, 0, 5), ("za", 3, 1, 6), ("za", 2, 1, 5), ("ye", 4), ("yr", 11), ("yo", 12), ("za", 1, 0, 6),
    ("za", 0, 0, 7), ("yo", 11), ("yr", 6), ("za", 1, 1, 6), ("yo", 10), ("yo", 6), ("yr", 9), ("g", 12),
    ("za", 3, 0, 7), ("za", 2, 0, 6), ("zb", 2, 8), ("yr", 10), ("za", 2, 1, 6), ("za", 0, 1, 7), ("za", 3, 1, 7),
    ("yr", 7), ("za", 1, 1, 7), ("yo", 7), ("ye", 11), ("ye", 6), ("ye", 5), ("g", 11), ("g", 5), ("g", 4),
    ("za", 1, 0, 7), ("za", 2, 0, 7), ("yr", 8), ("ye", 10), ("yo", 8), ("yo", 9), ("za", 3, 0, 8), ("za", 0, 1, 8),
    ("ye", 7), ("ye", 9), ("za", 2, 1, 7), ("g", 10), ("g", 6), ("g", 7), ("g", 9), ("za", 1, 1, 8), ("za", 2, 0, 8),
    ("ye", 8), ("g", 8),
)
MIRROR = True
LATE = 0


def order_tables(dst, src, count):
    n = SLOTS
    i32 = jnp.int32
    row = lax.broadcasted_iota(i32, (n, n), 0)
    col = lax.broadcasted_iota(i32, (n, n), 1)
    lane = lax.broadcasted_iota(i32, (1, n), 1)
    key_row = jnp.where(lane < count, dst * NREP + src, CELLS)
    key = jnp.sum(jnp.where(row == col, key_row, 0), axis=1, keepdims=True)
    before = (key_row < key) | ((key_row == key) & (col < row))
    place = jnp.sum(jnp.where(before, 1, 0), axis=1, keepdims=True)
    lanes = lax.broadcasted_iota(i32, (n, B), 1)
    slot = lax.broadcasted_iota(i32, (n, B), 0)
    rows = []
    for part in range(CELLS // B):
        last = jnp.max(jnp.where(key == lanes + part * B, place, -1), axis=0, keepdims=True)
        rows.append(jnp.where(last < 0, SLOTS, last))
    here = place == lanes
    rows.append(jnp.sum(jnp.where(here, slot, 0), axis=0, keepdims=True))
    mine = jnp.sum(jnp.where(here, key, 0), axis=0, keepdims=True)
    prior = jnp.sum(jnp.where(place + 1 == lanes, key, 0), axis=0, keepdims=True)
    rows.append(jnp.where((mine == prior) & (lanes[:1] > 0), 1, 0))
    return rows


def kernel(
    features,
    tiles_hbm,
    dst_hbm,
    src_hbm,
    count_ref,
    weights_hbm,
    biases_hbm,
    out,
    held,
    tiles,
    merged,
    dst_ref,
    src_ref,
    weights,
    biases,
    table_v,
    table,
    total,
    outbox,
    inbox,
    sent_sems,
    recv_sems,
    local_sems,
):
    rep = lax.axis_index("rep")
    me = lax.axis_index("loop")
    z = rep // NY
    y = rep % NY
    face = 1 - 2 * (lax.rem(z, 4) // 2) if MIRROR else 1

    def zmod(v):
        return lax.rem(v + 2 * NZ, NZ)

    def ymod(v):
        return lax.rem(v + 2 * NY, NY)

    def at(zz, yy):
        return {"rep": zz * NY + yy}

    y_up, y_down, y_far = at(z, ymod(y + 1)), at(z, ymod(y - 1)), at(z, ymod(y + 2))
    mates = [{"loop": lax.rem(me + d, NL)} for d in range(1, NL)]

    barrier = pltpu.get_barrier_semaphore()
    everyone = [at(zmod(z + 1), y), at(zmod(z - 1), y), y_up, y_down, y_far] + mates
    for other in everyone:
        pl.semaphore_signal(barrier, inc=1, device_id=other, device_id_type=MESH)

    copies = [
        pltpu.make_async_copy(a, b, local_sems.at[i])
        for i, (a, b) in enumerate(
            (
                (features, held.at[rep]),
                (dst_hbm, dst_ref),
                (src_hbm, src_ref),
                (tiles_hbm, tiles),
                (weights_hbm, weights),
                (biases_hbm, biases),
            )
        )
    ]
    for copy in copies:
        copy.start()
    own_in, dst_in, src_in, tiles_in, *later_in = copies
    table_in = pltpu.make_async_copy(table_v, table, local_sems.at[len(copies)])

    def tables():
        merged[SLOTS] = jnp.zeros((B, B), jnp.bfloat16)
        dst_in.wait()
        src_in.wait()
        table_v[...] = jnp.zeros_like(table_v)
        for i, row in enumerate(order_tables(dst_ref[...], src_ref[...], count_ref[0])):
            table_v[pl.ds(i, 1), :] = row
        table_in.start()
        tiles_in.wait()
        table_in.wait()

    def merge():
        def step(i, run):
            for q in range(4):
                q = 4 * i + q
                run = jnp.where(table[5, q] > 0, run, 0.0) + tiles[table[4, q]].astype(jnp.float32)
                merged[q] = run.astype(jnp.bfloat16)
            return run

        lax.fori_loop(0, SLOTS // 4, step, jnp.zeros((B, B), jnp.float32))

    def partial_copy(k, d):
        return pltpu.make_async_remote_copy(
            src_ref=outbox.at[k * NL + d],
            dst_ref=inbox.at[k * NL + d],
            send_sem=sent_sems.at[LAYERS + k],
            recv_sem=recv_sems.at[k * NSEM + RS + d],
            device_id=mates[d - 1],
            device_id_type=MESH,
        )

    def layer(k, unused):
        def link(ref, sem, device):
            return pltpu.make_async_remote_copy(
                src_ref=ref,
                dst_ref=ref,
                send_sem=sent_sems.at[k],
                recv_sem=recv_sems.at[k * NSEM + sem],
                device_id=device,
                device_id_type=MESH,
            )

        def send(ref, sem, device):
            link(ref, sem, device).start()

        def landed(ref, sem):
            link(ref, sem, y_up).wait_recv()

        def block(off, dy):
            return k * NREP + zmod(z + off) * NY + ymod(y + dy)

        def rows_a(off, dy):
            return held.at[block(off, dy), pl.ds(0, RA), :]

        def rows_b(off, dy=0, part=None):
            if part is None:
                return held.at[block(off, dy), pl.ds(RA, RB), :]
            return held.at[block(off, dy), pl.ds(RA, CUT) if part else pl.ds(RA + CUT, RB - CUT), :]

        def sem_zb(way, i):
            return ZB + (1 - way) // 2 * (HALF + 1) + i

        def sem_za(dy, way, i):
            return ZA + (2 * dy + (1 - way) // 2) * (HALF + 1) + i

        def send_b(way, i):
            ref = rows_b(-way * (i - 1), 0, None if i < HALF else way > 0)
            send(ref, sem_zb(way, i), at(zmod(z + way), y))

        def send_a(dy, way, i):
            send(rows_a(-way * (i - 1), dy), sem_za(dy, way, i), at(zmod(z + way), y))

        def sem_yb(kind, off):
            return YB + kind * NZ + zmod(off)

        def y_send(off):
            send(rows_b(off), sem_yb(0, off), y_up)
            send(rows_b(off), sem_yb(1, off), y_down)

        def turned(off):
            off = off if off <= HALF else off - NZ
            return off * face if abs(off) < HALF - 1 else off

        def from_y(off, up):
            landed(rows_b(off, -1 if up else 1), sem_yb(0 if up else 1, off))

        def group(off):
            zz = zmod(z + off) * NY
            right = held[pl.ds(k * NREP + zz, NY)].reshape(NY * B, F)

            def product(d):
                cell = lax.rem(me + d, NL) * NREP + zz
                line, at0 = cell // B, lax.rem(cell, B)
                left = jnp.concatenate([merged[table[line, at0 + yy]] for yy in range(NY)], axis=1)
                return jnp.dot(left, right, preferred_element_type=jnp.float32)

            return product

        def handle(step):
            kind, *which = step
            if kind == "zb" and which[1] == HALF:
                for way in (1, -1):
                    landed(rows_b(HALF, 0, way > 0), sem_zb(way, HALF))
                y_send(HALF)
            elif kind == "zb":
                up, i = which
                way = (1 if up else -1) * (face if i < HALF - 1 else 1)
                landed(rows_b(-way * i), sem_zb(way, i))
                send_b(way, i + 1)
                y_send(-way * i)
            elif kind == "za":
                dy, up, i = which
                way = (1 if up else -1) * (face if i < HALF - 1 else 1)
                landed(rows_a(-way * i, dy), sem_za(dy, way, i))
                if i < HALF - 1 or (i == HALF - 1 and up == (dy < 2)):
                    send_a(dy, way, i + 1)
            elif kind == "ya":
                dy = which[0]
                landed(rows_a(0, dy), YA + NY - dy)
                send_a(dy, 1, 1)
                send_a(dy, -1, 1)
            elif kind in ("yr", "yo"):
                even = which[0] % 2 == 0
                off = turned(which[0])
                from_y(off, even == (kind == "yr"))
                if kind == "yr":
                    send(rows_b(off, -1 if even else 1), sem_yb(2, off), y_up if even else y_down)
            elif kind == "ye":
                off = turned(which[0])
                landed(rows_b(off, 2), sem_yb(2, off))

        for way in (1, -1):
            send_b(way, 1)
        for way in (1, -1):
            send_a(0, way, 1)
        for dy, device in ((1, y_up), (3, y_down), (2, y_far)):
            send(rows_a(0, 0), YA + dy, device)
        y_send(0)

        @pl.when(k == 0)
        def _():
            tables()
            merge()
            for copy in later_in:
                copy.wait()

        begun = False
        late = []
        final = max(n for n, step in enumerate(ORDER) if step[0] != "g")
        for n, step in enumerate(ORDER):
            if step[0] != "g":
                handle(step)
            elif n > final or n > len(ORDER) - LATE:
                late.append(turned(step[1]))
            else:
                product = group(turned(step[1]))
                for d in range(NL):
                    part = product(d)
                    total[d] = total[d] + part if begun else part
                begun = True
        late = [group(off) for off in late]
        for d in (4, 3, 5, 2, 6, 1, 7, 0):
            part = total[d]
            for product in late:
                part = part + product(d)
            if d:
                outbox[k * NL + d] = part.astype(jnp.bfloat16)
                partial_copy(k, d).start()
        for d in (1, 7, 2, 6, 3, 5, 4):
            partial_copy(k, d).wait_recv()
            part = part + inbox[k * NL + d].astype(jnp.float32)
        mixed = jnp.dot(part.astype(jnp.bfloat16), weights[k], preferred_element_type=jnp.float32)
        hidden = jnp.maximum(mixed + biases[pl.ds(k, 1), :], 0.0).astype(jnp.bfloat16)

        @pl.when(k + 1 < LAYERS)
        def _():
            held[(k + 1) * NREP + rep] = hidden

        @pl.when(k + 1 == LAYERS)
        def _():
            out[...] = hidden

        return unused

    own_in.wait()
    pl.semaphore_wait(barrier, len(everyone))
    lax.fori_loop(0, LAYERS, layer, 0)
    for k in range(LAYERS):
        for buffer, sem, blocks in ((held, k, NREP - 1), (outbox, LAYERS + k, NL - 1)):
            whole = buffer.at[pl.ds(0, blocks)]
            pltpu.make_async_remote_copy(
                src_ref=whole,
                dst_ref=whole,
                send_sem=sent_sems.at[sem],
                recv_sem=recv_sems.at[0],
                device_id=y_up,
                device_id_type=MESH,
            ).wait_send()


def body(features, tiles, tile_dst, tile_src, tile_count, weights, biases):
    vmem, anyspace = pl.BlockSpec(memory_space=pltpu.VMEM), pl.BlockSpec(memory_space=pl.ANY)
    smem = pl.BlockSpec(memory_space=pltpu.SMEM)
    return pl.pallas_call(
        kernel,
        out_shape=jax.ShapeDtypeStruct((B, F), jnp.bfloat16),
        in_specs=[anyspace, anyspace, anyspace, anyspace, smem, anyspace, anyspace],
        out_specs=vmem,
        scratch_shapes=[
            pltpu.VMEM((LAYERS * NREP, B, F), jnp.bfloat16),
            pltpu.VMEM((SLOTS, B, B), jnp.bfloat16),
            pltpu.VMEM((SLOTS + 1, B, B), jnp.bfloat16),
            pltpu.VMEM((1, SLOTS), jnp.int32),
            pltpu.VMEM((1, SLOTS), jnp.int32),
            pltpu.VMEM((LAYERS, F, F), jnp.bfloat16),
            pltpu.VMEM((LAYERS, F), jnp.float32),
            pltpu.VMEM((8, B), jnp.int32),
            pltpu.SMEM((8, B), jnp.int32),
            pltpu.VMEM((NL, B, F), jnp.float32),
            pltpu.VMEM((LAYERS * NL, B, F), jnp.bfloat16),
            pltpu.VMEM((LAYERS * NL, B, F), jnp.bfloat16),
            pltpu.SemaphoreType.DMA((2 * LAYERS,)),
            pltpu.SemaphoreType.DMA((LAYERS * NSEM,)),
            pltpu.SemaphoreType.DMA((8,)),
        ],
        compiler_params=pltpu.CompilerParams(
            collective_id=0, has_side_effects=True, vmem_limit_bytes=VMEM
        ),
        cost_estimate=pl.CostEstimate(flops=2 * LAYERS * CELLS * B * B * F, bytes_accessed=4 << 20, transcendentals=0),
    )(
        features,
        tiles,
        tile_dst.reshape(1, SLOTS),
        tile_src.reshape(1, SLOTS),
        tile_count,
        weights,
        biases,
    )


def solution(mesh):
    in_specs = (
        P(("rep", "loop"), None),
        P(("rep", "loop"), None, None),
        P(("rep", "loop")),
        P(("rep", "loop")),
        P(("rep", "loop")),
        P(),
        P(),
    )
    out_specs = P(("rep", "loop"), None)
    return jax.shard_map(body, mesh=mesh, in_specs=in_specs, out_specs=out_specs, check_vma=False)
```

time: 465 us -> 103 us (0.22)
  waiting for transfers between devices: 369 us -> 0 us
  Pallas kernels: 0 us -> 100 us
  local copies, waits for them, and re-layouts: 37.2 us -> 1.47 us
  matrix products: 30.1 us -> 0 us
  other arithmetic: 12.8 us -> 0 us
  between operations: 13.2 us -> 0.66 us
    all_gather x2 -> x0, waiting for transfers between devices: 287 us -> none  [one_layer(): gathered = lax.all_gather(hidden, 'rep', axis=0, tiled=True)]
    pallas_call x0 -> x1, Pallas kernels: none -> 100 us  [body(): pl.pallas_call(kernel, out_shape=jax.ShapeDtypeStruct((B, F), jnp.bfloat1...]
    reduce_scatter x2 -> x0, waiting for transfers between devices: 81.3 us -> none  [one_layer(): lax.psum_scatter(partial_value, 'loop', scatter_dimension=0, tiled=True)]
    gather x12 -> x0, local copies, waits for them, and re-layouts: 33.6 us -> none  [accumulate(): src_rows = blocks[src_group]]
    dot_general x26 -> x0, matrix products: 30.1 us -> none  [the longest x12 17.6 us: accumulate(): jnp.einsum('tab,tbf->taf', tile_group, src_rows, preferred_element_type=j...]
    lt x12 -> x0, other arithmetic: 7.81 us -> none  [accumulate(): valid = start + jnp.arange(group, dtype=jnp.int32) < occupied]
    select_n x12 -> x0, other arithmetic: 4.89 us -> none  [accumulate(): src_rows = blocks[src_group]]
  transfers between devices with their start and end apart: 4 -> 0, of which waited for: 4 -> 0; matrix products, arithmetic and copies ran while one was open for 0% -> 0% of each run, Pallas kernels for 0% -> 0%
where the time goes in v3:
time: 103 us; the launch traced here: 102 us
  Pallas kernels  100 us (97%)
  local copies, waits for them, and re-layouts  1.47 us (1%)
    pallas_call x1, Pallas kernels, body(): pl.pallas_call(kernel, out_shape=jax.ShapeDtypeStruct((B, F), jnp.bfloat1...  100 us

profile of v3, /device:TPU:1, one launch (start us, length us, event | category | flops | bytes accessed | tf_op | source)
XLA Modules:
  0.0 102.4 jit_solution(4512441336018415059)
XLA Ops:
  0.7 100.3 %shard_map.73 = bf16[128,256]{1,0:T(8,128)(2,1)} custom-call(bf16[128,256]{1,0:T(8,128)(2,1)} %features.1, bf16[96,128,128]{2,1,0:T(8,128)(2,1)} %tiles_hbm.1, s32[1,96]{1,0:T(1,128)} %bitcast.2, s32[1,96]{1,0:T(1,128)} %bitcast.3, s32[1]{0:T(128)S(6)} %copy.9.count_ref, bf16[2,256,256]{2,1,0:T(8,128)(2,1)} %weights_hbm.1, f32[2,256]{1,0:T(2,128)} %biases_hbm.1), custom_call_target="tpu_custom_call" | custom-call | flops 8589934592 | bytes 4194304 | tf_op jit(solution)/shard_map/pallas_call | solution.py:344
  100.9 1.5 %copy.10 = bf16[128,256]{1,0:T(8,128)(2,1)} copy(bf16[128,256]{1,0:T(8,128)(2,1)} %shard_map.73) | data formatting | bytes 131072

commit v4 on v3

--- a/solution.py
+++ b/solution.py
@@ -18,34 +18,72 @@
 VMEM = 62 * 1024 * 1024
 HALF = NZ // 2
 CELLS = NL * NREP
-ZB, ZA = 0, 2 * (HALF + 1)
+ZB, ZA = 0, 4 * (HALF + 1)
 YA = ZA + NY * 2 * (HALF + 1)
 YB = YA + NY
 RS = YB + 3 * NZ
 NSEM = RS + NL
 ORDER = (
-    ("zb", 0, 1), ("zb", 1, 1), ("za", 0, 0, 1), ("ya", 3), ("ya", 1), ("za", 0, 1, 1), ("zb", 0, 2), ("zb", 1, 2),
-    ("yo", 0), ("za", 3, 0, 1), ("ya", 2), ("yr", 15), ("za", 3, 1, 1), ("za", 1, 1, 1), ("za", 1, 0, 1), ("yr", 0),
-    ("za", 0, 0, 2), ("za", 0, 1, 2), ("zb", 1, 3), ("zb", 0, 3), ("za", 2, 0, 1), ("za", 3, 1, 2), ("za", 3, 0, 2),
-    ("yo", 14), ("yr", 1), ("za", 2, 1, 1), ("za", 1, 0, 2), ("yo", 2), ("za", 1, 1, 2), ("yo", 15), ("yr", 2),
-    ("za", 0, 0, 3), ("za", 0, 1, 3), ("yr", 14), ("yr", 13), ("zb", 0, 4), ("zb", 1, 4), ("za", 2, 1, 2),
-    ("za", 3, 0, 3), ("za", 3, 1, 3), ("za", 1, 0, 3), ("za", 1, 1, 3), ("ye", 15), ("za", 2, 0, 2), ("yr", 3),
-    ("g", 15), ("za", 0, 0, 4), ("ye", 0), ("za", 0, 1, 4), ("ye", 1), ("yo", 1), ("yo", 13), ("zb", 0, 5),
-    ("zb", 1, 5), ("za", 3, 1, 4), ("za", 3, 0, 4), ("ye", 2), ("g", 0), ("za", 2, 0, 3), ("za", 1, 0, 4),
-    ("za", 1, 1, 4), ("g", 1), ("ye", 13), ("za", 2, 1, 3), ("za", 0, 0, 5), ("yr", 12), ("ye", 14), ("yr", 4),
-    ("za", 0, 1, 5), ("zb", 0, 6), ("zb", 1, 6), ("g", 14), ("yo", 5), ("yo", 3), ("za", 1, 0, 5), ("za", 3, 1, 5),
-    ("yo", 4), ("za", 3, 0, 5), ("za", 2, 0, 4), ("ye", 3), ("za", 2, 1, 4), ("za", 1, 1, 5), ("yr", 5),
-    ("za", 0, 0, 6), ("g", 13), ("ye", 12), ("zb", 1, 7), ("za", 0, 1, 6), ("g", 3), ("zb", 0, 7), ("za", 3, 0, 6),
-    ("g", 2), ("za", 2, 0, 5), ("za", 3, 1, 6), ("za", 2, 1, 5), ("ye", 4), ("yr", 11), ("yo", 12), ("za", 1, 0, 6),
-    ("za", 0, 0, 7), ("yo", 11), ("yr", 6), ("za", 1, 1, 6), ("yo", 10), ("yo", 6), ("yr", 9), ("g", 12),
-    ("za", 3, 0, 7), ("za", 2, 0, 6), ("zb", 2, 8), ("yr", 10), ("za", 2, 1, 6), ("za", 0, 1, 7), ("za", 3, 1, 7),
-    ("yr", 7), ("za", 1, 1, 7), ("yo", 7), ("ye", 11), ("ye", 6), ("ye", 5), ("g", 11), ("g", 5), ("g", 4),
-    ("za", 1, 0, 7), ("za", 2, 0, 7), ("yr", 8), ("ye", 10), ("yo", 8), ("yo", 9), ("za", 3, 0, 8), ("za", 0, 1, 8),
-    ("ye", 7), ("ye", 9), ("za", 2, 1, 7), ("g", 10), ("g", 6), ("g", 7), ("g", 9), ("za", 1, 1, 8), ("za", 2, 0, 8),
-    ("ye", 8), ("g", 8),
+    ("s", "ya", 1), ("s", "zb", 1, 1, 0), ("s", "zb", 0, 1, 0), ("s", "zb", 1, 1, 1), ("s", "zb", 0, 1, 1),
+    ("s", "za", 0, 0, 1), ("s", "ya", 3), ("s", "za", 0, 1, 1), ("s", "ya", 2), ("w", "zb", 0, 1, 0),
+    ("s", "zb", 0, 2, 0), ("w", "zb", 0, 1, 1), ("w", "zb", 1, 1, 0), ("s", "zb", 1, 2, 0), ("s", "zb", 0, 2, 1),
+    ("w", "ya", 1), ("s", "za", 3, 0, 1), ("w", "ya", 3), ("s", "yb", 1, 1, 2), ("w", "za", 0, 0, 1),
+    ("w", "zb", 1, 1, 1), ("s", "zb", 1, 2, 1), ("s", "yb", 1, 0, 2), ("s", "za", 3, 1, 1), ("w", "za", 0, 1, 1),
+    ("s", "za", 1, 0, 1), ("s", "za", 1, 1, 1), ("s", "yb", 0, 1, 2), ("s", "za", 0, 1, 2), ("s", "yb", 1, 15, 2),
+    ("s", "za", 0, 0, 2), ("w", "zb", 0, 2, 0), ("s", "zb", 0, 3, 0), ("w", "zb", 1, 2, 0), ("s", "zb", 1, 3, 0),
+    ("w", "zb", 0, 2, 1), ("s", "yb", 0, 0, 2), ("s", "zb", 0, 3, 1), ("w", "zb", 1, 2, 1), ("s", "zb", 1, 3, 1),
+    ("s", "yb", 0, 14, 2), ("w", "za", 3, 0, 1), ("w", "za", 3, 1, 1), ("s", "za", 3, 0, 2), ("s", "za", 3, 1, 2),
+    ("w", "za", 1, 0, 1), ("w", "ya", 2), ("s", "za", 2, 0, 1), ("s", "za", 2, 1, 1), ("w", "yb", 1, 1, 2),
+    ("w", "za", 1, 1, 1), ("s", "za", 1, 0, 2), ("s", "za", 1, 1, 2), ("w", "za", 0, 1, 2), ("w", "za", 0, 0, 2),
+    ("s", "yb", 0, 2, 2), ("s", "yb", 1, 14, 2), ("w", "zb", 0, 3, 0), ("s", "za", 0, 1, 3), ("s", "zb", 0, 4, 0),
+    ("s", "za", 0, 0, 3), ("w", "zb", 1, 3, 0), ("w", "yb", 1, 15, 2), ("s", "yb", 0, 15, 2), ("s", "yb", 2, 15, 2),
+    ("s", "zb", 1, 4, 0), ("w", "zb", 1, 3, 1), ("w", "zb", 0, 3, 1), ("s", "zb", 0, 4, 1), ("s", "zb", 1, 4, 1),
+    ("w", "za", 3, 1, 2), ("s", "za", 3, 1, 3), ("w", "za", 2, 0, 1), ("s", "za", 2, 0, 2), ("s", "yb", 0, 13, 2),
+    ("s", "yb", 2, 1, 2), ("w", "za", 3, 0, 2), ("w", "za", 1, 0, 2), ("s", "za", 3, 0, 3), ("w", "za", 2, 1, 1),
+    ("w", "yb", 0, 0, 2), ("s", "za", 2, 1, 2), ("w", "za", 1, 1, 2), ("s", "za", 1, 0, 3), ("s", "yb", 1, 3, 2),
+    ("s", "za", 1, 1, 3), ("s", "yb", 1, 13, 2), ("w", "zb", 0, 4, 0), ("s", "zb", 0, 5, 0), ("s", "yb", 2, 0, 2),
+    ("w", "zb", 1, 4, 0), ("s", "zb", 1, 5, 0), ("w", "za", 0, 0, 3), ("w", "zb", 0, 4, 1), ("s", "zb", 0, 5, 1),
+    ("s", "za", 0, 0, 4), ("s", "yb", 1, 2, 2), ("w", "za", 0, 1, 3), ("w", "zb", 1, 4, 1), ("s", "zb", 1, 5, 1),
+    ("s", "za", 0, 1, 4), ("s", "yb", 0, 4, 2), ("w", "za", 2, 0, 2), ("s", "za", 2, 0, 3), ("w", "za", 2, 1, 2),
+    ("w", "za", 3, 0, 3), ("s", "za", 2, 1, 3), ("s", "za", 3, 0, 4), ("s", "yb", 0, 3, 2), ("w", "za", 3, 1, 3),
+    ("s", "za", 3, 1, 4), ("w", "yb", 0, 2, 2), ("s", "yb", 0, 12, 2), ("w", "za", 1, 0, 3), ("s", "yb", 1, 4, 2),
+    ("w", "yb", 0, 14, 2), ("s", "za", 1, 0, 4), ("w", "za", 1, 1, 3), ("s", "za", 1, 1, 4), ("w", "zb", 0, 5, 0),
+    ("s", "zb", 0, 6, 0), ("w", "yb", 0, 1, 2), ("w", "zb", 1, 5, 0), ("s", "zb", 1, 6, 0), ("w", "zb", 0, 5, 1),
+    ("s", "yb", 1, 12, 2), ("s", "zb", 0, 6, 1), ("s", "yb", 2, 2, 2), ("w", "zb", 1, 5, 1), ("s", "zb", 1, 6, 1),
+    ("w", "za", 0, 0, 4), ("w", "yb", 2, 0, 2), ("s", "za", 0, 0, 5), ("s", "yb", 2, 14, 2), ("w", "za", 0, 1, 4),
+    ("s", "za", 0, 1, 5), ("w", "yb", 2, 15, 2), ("w", "yb", 1, 3, 2), ("s", "yb", 1, 5, 2), ("s", "yb", 0, 5, 2),
+    ("w", "za", 2, 0, 3), ("s", "za", 2, 0, 4), ("w", "za", 2, 1, 3), ("s", "za", 2, 1, 4), ("w", "za", 3, 0, 4),
+    ("w", "za", 1, 0, 4), ("s", "za", 1, 0, 5), ("s", "yb", 2, 3, 2), ("w", "za", 3, 1, 4), ("w", "za", 1, 1, 4),
+    ("s", "za", 3, 0, 5), ("w", "yb", 0, 12, 2), ("s", "za", 1, 1, 5), ("s", "za", 3, 1, 5), ("s", "yb", 1, 11, 2),
+    ("w", "yb", 0, 3, 2), ("w", "zb", 0, 6, 0), ("s", "yb", 2, 12, 2), ("w", "yb", 2, 1, 2), ("w", "yb", 1, 14, 2),
+    ("w", "zb", 1, 6, 0), ("s", "zb", 0, 7, 0), ("s", "zb", 1, 7, 0), ("w", "yb", 0, 15, 2), ("w", "zb", 0, 6, 1),
+    ("w", "zb", 1, 6, 1), ("s", "yb", 1, 10, 2), ("s", "zb", 0, 7, 1), ("w", "yb", 1, 13, 2), ("s", "zb", 1, 7, 1),
+    ("w", "yb", 1, 2, 2), ("s", "yb", 1, 6, 2), ("w", "za", 0, 0, 5), ("s", "yb", 2, 13, 2), ("s", "yb", 0, 6, 2),
+    ("w", "za", 2, 0, 4), ("s", "za", 2, 0, 5), ("s", "yb", 0, 10, 2), ("w", "za", 2, 1, 4), ("s", "za", 2, 1, 5),
+    ("s", "za", 0, 0, 6), ("g", 15), ("w", "za", 0, 1, 5), ("s", "za", 0, 1, 6), ("w", "yb", 1, 12, 2),
+    ("s", "yb", 0, 11, 2), ("w", "yb", 0, 4, 2), ("w", "za", 1, 0, 5), ("s", "za", 1, 0, 6), ("w", "za", 1, 1, 5),
+    ("s", "za", 1, 1, 6), ("w", "yb", 1, 5, 2), ("w", "yb", 2, 2, 2), ("g", 2), ("w", "za", 3, 0, 5),
+    ("w", "yb", 2, 3, 2), ("s", "za", 3, 0, 6), ("w", "za", 3, 1, 5), ("s", "za", 3, 1, 6), ("s", "yb", 2, 4, 2),
+    ("s", "yb", 2, 5, 2), ("w", "zb", 1, 7, 0), ("w", "yb", 1, 4, 2), ("s", "zb", 1, 8, 0), ("w", "zb", 0, 7, 1),
+    ("s", "zb", 0, 8, 1), ("g", 3), ("w", "za", 2, 0, 5), ("s", "za", 2, 0, 6), ("w", "zb", 1, 7, 1),
+    ("w", "za", 2, 1, 5), ("s", "yb", 1, 9, 2), ("s", "za", 2, 1, 6), ("w", "yb", 0, 6, 2), ("w", "yb", 1, 11, 2),
+    ("s", "yb", 0, 9, 2), ("w", "za", 0, 0, 6), ("w", "zb", 0, 7, 0), ("w", "za", 0, 1, 6), ("s", "yb", 1, 7, 2),
+    ("s", "yb", 2, 6, 2), ("w", "yb", 1, 0, 2), ("w", "yb", 2, 14, 2), ("s", "za", 0, 1, 7), ("g", 0),
+    ("w", "yb", 0, 5, 2), ("w", "za", 1, 1, 6), ("w", "yb", 2, 12, 2), ("w", "za", 1, 0, 6), ("s", "za", 1, 1, 7),
+    ("s", "za", 1, 0, 7), ("g", 14), ("w", "za", 3, 1, 6), ("w", "za", 3, 0, 6), ("s", "za", 3, 0, 7),
+    ("s", "yb", 2, 11, 2), ("w", "yb", 1, 10, 2), ("w", "yb", 0, 13, 2), ("s", "za", 3, 1, 7), ("w", "yb", 1, 6, 2),
+    ("w", "zb", 1, 8, 0), ("w", "yb", 2, 13, 2), ("w", "zb", 0, 8, 1), ("s", "za", 0, 0, 7), ("s", "yb", 0, 8, 2),
+    ("s", "yb", 1, 8, 2), ("w", "yb", 0, 10, 2), ("g", 12), ("s", "yb", 2, 10, 2), ("w", "za", 2, 0, 6),
+    ("w", "za", 2, 1, 6), ("s", "za", 2, 0, 7), ("w", "yb", 2, 4, 2), ("g", 4), ("w", "yb", 2, 5, 2),
+    ("s", "za", 2, 1, 7), ("s", "yb", 0, 7, 2), ("w", "yb", 1, 9, 2), ("s", "yb", 2, 9, 2), ("g", 13), ("g", 5),
+    ("w", "za", 0, 1, 7), ("w", "yb", 0, 9, 2), ("w", "yb", 1, 7, 2), ("w", "za", 1, 1, 7), ("s", "za", 1, 1, 8),
+    ("s", "za", 0, 1, 8), ("s", "yb", 2, 7, 2), ("w", "yb", 2, 6, 2), ("w", "za", 3, 0, 7), ("s", "za", 3, 0, 8),
+    ("w", "za", 1, 0, 7), ("g", 6), ("w", "yb", 0, 8, 2), ("s", "yb", 2, 8, 2), ("w", "za", 2, 0, 7),
+    ("s", "za", 2, 0, 8), ("w", "za", 0, 0, 7), ("w", "za", 3, 1, 7), ("w", "yb", 2, 11, 2), ("w", "yb", 0, 11, 2),
+    ("g", 1), ("w", "yb", 2, 10, 2), ("g", 10), ("w", "za", 2, 1, 7), ("g", 11), ("w", "yb", 2, 9, 2), ("g", 9),
+    ("w", "yb", 0, 7, 2), ("w", "yb", 1, 8, 2), ("w", "za", 3, 0, 8), ("w", "za", 1, 1, 8), ("w", "yb", 2, 7, 2),
+    ("g", 7), ("w", "za", 0, 1, 8), ("w", "yb", 2, 8, 2), ("w", "za", 2, 0, 8), ("g", 8),
 )
-MIRROR = True
-LATE = 0
 
 
 def order_tables(dst, src, count):
@@ -101,7 +139,7 @@
     me = lax.axis_index("loop")
     z = rep // NY
     y = rep % NY
-    face = 1 - 2 * (lax.rem(z, 4) // 2) if MIRROR else 1
+    face = 1 - 2 * (lax.rem(z, 4) // 2)
 
     def zmod(v):
         return lax.rem(v + 2 * NZ, NZ)
@@ -197,32 +235,35 @@
                 return held.at[block(off, dy), pl.ds(RA, RB), :]
             return held.at[block(off, dy), pl.ds(RA, CUT) if part else pl.ds(RA + CUT, RB - CUT), :]
 
-        def sem_zb(way, i):
-            return ZB + (1 - way) // 2 * (HALF + 1) + i
-
-        def sem_za(dy, way, i):
-            return ZA + (2 * dy + (1 - way) // 2) * (HALF + 1) + i
-
-        def send_b(way, i):
-            ref = rows_b(-way * (i - 1), 0, None if i < HALF else way > 0)
-            send(ref, sem_zb(way, i), at(zmod(z + way), y))
-
-        def send_a(dy, way, i):
-            send(rows_a(-way * (i - 1), dy), sem_za(dy, way, i), at(zmod(z + way), y))
-
-        def sem_yb(kind, off):
-            return YB + kind * NZ + zmod(off)
-
-        def y_send(off):
-            send(rows_b(off), sem_yb(0, off), y_up)
-            send(rows_b(off), sem_yb(1, off), y_down)
+        def towards(up, i):
+            return (1 if up else -1) * (face if i < HALF - 1 else 1)
 
         def turned(off):
             off = off if off <= HALF else off - NZ
             return off * face if abs(off) < HALF - 1 else off
 
-        def from_y(off, up):
-            landed(rows_b(off, -1 if up else 1), sem_yb(0 if up else 1, off))
+        def piece(what, leaving):
+            kind, *which = what
+            if kind == "zb":
+                up, i, part = which
+                way = towards(up, i)
+                ref = rows_b(-way * (i - leaving), 0, None if part == 2 else part == 0)
+                return ref, ZB + (2 * (part % 2) + (1 - way) // 2) * (HALF + 1) + i, at(zmod(z + way), y)
+            if kind == "za":
+                dy, up, i = which
+                way = towards(up, i)
+                sem = ZA + (2 * dy + (1 - way) // 2) * (HALF + 1) + i
+                return rows_a(-way * (i - leaving), dy), sem, at(zmod(z + way), y)
+            if kind == "ya":
+                dy = which[0]
+                return rows_a(0, 0 if leaving else -dy), YA + dy, (None, y_up, y_far, y_down)[dy]
+            hop, place, _ = which
+            off = turned(place)
+            up = hop == 0 or (hop == 2 and place % 2 == 0)
+            sem = YB + hop * NZ + zmod(off)
+            if hop == 2:
+                return rows_b(off, (-1 if up else 1) if leaving else 2), sem, y_up if up else y_down
+            return rows_b(off, 0 if leaving else (-1 if up else 1)), sem, y_up if up else y_down
 
         def group(off):
             zz = zmod(z + off) * NY
@@ -236,46 +277,16 @@
 
             return product
 
-        def handle(step):
-            kind, *which = step
-            if kind == "zb" and which[1] == HALF:
-                for way in (1, -1):
-                    landed(rows_b(HALF, 0, way > 0), sem_zb(way, HALF))
-                y_send(HALF)
-            elif kind == "zb":
-                up, i = which
-                way = (1 if up else -1) * (face if i < HALF - 1 else 1)
-                landed(rows_b(-way * i), sem_zb(way, i))
-                send_b(way, i + 1)
-                y_send(-way * i)
-            elif kind == "za":
-                dy, up, i = which
-                way = (1 if up else -1) * (face if i < HALF - 1 else 1)
-                landed(rows_a(-way * i, dy), sem_za(dy, way, i))
-                if i < HALF - 1 or (i == HALF - 1 and up == (dy < 2)):
-                    send_a(dy, way, i + 1)
-            elif kind == "ya":
-                dy = which[0]
-                landed(rows_a(0, dy), YA + NY - dy)
-                send_a(dy, 1, 1)
-                send_a(dy, -1, 1)
-            elif kind in ("yr", "yo"):
-                even = which[0] % 2 == 0
-                off = turned(which[0])
-                from_y(off, even == (kind == "yr"))
-                if kind == "yr":
-                    send(rows_b(off, -1 if even else 1), sem_yb(2, off), y_up if even else y_down)
-            elif kind == "ye":
-                off = turned(which[0])
-                landed(rows_b(off, 2), sem_yb(2, off))
-
-        for way in (1, -1):
-            send_b(way, 1)
-        for way in (1, -1):
-            send_a(0, way, 1)
-        for dy, device in ((1, y_up), (3, y_down), (2, y_far)):
-            send(rows_a(0, 0), YA + dy, device)
-        y_send(0)
+        def take(step):
+            ref, sem, device = piece(step[1:], step[0] == "s")
+            if step[0] == "s":
+                send(ref, sem, device)
+            else:
+                landed(ref, sem)
+
+        opening = min(n for n, step in enumerate(ORDER) if step[0] == "w")
+        for step in ORDER[:opening]:
+            take(step)
 
         @pl.when(k == 0)
         def _():
@@ -286,11 +297,11 @@
 
         begun = False
         late = []
-        final = max(n for n, step in enumerate(ORDER) if step[0] != "g")
-        for n, step in enumerate(ORDER):
+        final = max(n for n, step in enumerate(ORDER) if step[0] == "w")
+        for n, step in enumerate(ORDER[opening:], opening):
             if step[0] != "g":
-                handle(step)
-            elif n > final or n > len(ORDER) - LATE:
+                take(step)
+            elif n > final:
                 late.append(turned(step[1]))
             else:
                 product = group(turned(step[1]))

time: 103 us -> 98 us (0.951)
  Pallas kernels: 100 us -> 95.7 us
    pallas_call x1, Pallas kernels: 100 us -> 95.7 us  [body(): pl.pallas_call(kernel, out_shape=jax.ShapeDtypeStruct((B, F), jnp.bfloat1...]
where the time goes in v4:
time: 98 us; the launch traced here: 97.9 us
  Pallas kernels  95.7 us (98%)
  local copies, waits for them, and re-layouts  1.47 us (2%)
    pallas_call x1, Pallas kernels, body(): pl.pallas_call(kernel, out_shape=jax.ShapeDtypeStruct((B, F), jnp.bfloat1...  95.7 us

profile of v4, /device:TPU:1, one launch (start us, length us, event | category | flops | bytes accessed | tf_op | source)
XLA Modules:
  0.0 97.9 jit_solution(15423082741998402419)
XLA Ops:
  0.7 95.7 %shard_map.73 = bf16[128,256]{1,0:T(8,128)(2,1)} custom-call(bf16[128,256]{1,0:T(8,128)(2,1)} %features.1, bf16[96,128,128]{2,1,0:T(8,128)(2,1)} %tiles_hbm.1, s32[1,96]{1,0:T(1,128)} %bitcast.2, s32[1,96]{1,0:T(1,128)} %bitcast.3, s32[1]{0:T(128)S(6)} %copy.9.count_ref, bf16[2,256,256]{2,1,0:T(8,128)(2,1)} %weights_hbm.1, f32[2,256]{1,0:T(2,128)} %biases_hbm.1), custom_call_target="tpu_custom_call" | custom-call | flops 8589934592 | bytes 4194304 | tf_op jit(solution)/shard_map/pallas_call | solution.py:355
  96.4 1.5 %copy.10 = bf16[128,256]{1,0:T(8,128)(2,1)} copy(bf16[128,256]{1,0:T(8,128)(2,1)} %shard_map.73) | data formatting | bytes 131072

commit v5 on v4

--- a/solution.py
+++ b/solution.py
@@ -24,65 +24,65 @@
 RS = YB + 3 * NZ
 NSEM = RS + NL
 ORDER = (
-    ("s", "ya", 1), ("s", "zb", 1, 1, 0), ("s", "zb", 0, 1, 0), ("s", "zb", 1, 1, 1), ("s", "zb", 0, 1, 1),
-    ("s", "za", 0, 0, 1), ("s", "ya", 3), ("s", "za", 0, 1, 1), ("s", "ya", 2), ("w", "zb", 0, 1, 0),
-    ("s", "zb", 0, 2, 0), ("w", "zb", 0, 1, 1), ("w", "zb", 1, 1, 0), ("s", "zb", 1, 2, 0), ("s", "zb", 0, 2, 1),
-    ("w", "ya", 1), ("s", "za", 3, 0, 1), ("w", "ya", 3), ("s", "yb", 1, 1, 2), ("w", "za", 0, 0, 1),
-    ("w", "zb", 1, 1, 1), ("s", "zb", 1, 2, 1), ("s", "yb", 1, 0, 2), ("s", "za", 3, 1, 1), ("w", "za", 0, 1, 1),
-    ("s", "za", 1, 0, 1), ("s", "za", 1, 1, 1), ("s", "yb", 0, 1, 2), ("s", "za", 0, 1, 2), ("s", "yb", 1, 15, 2),
-    ("s", "za", 0, 0, 2), ("w", "zb", 0, 2, 0), ("s", "zb", 0, 3, 0), ("w", "zb", 1, 2, 0), ("s", "zb", 1, 3, 0),
-    ("w", "zb", 0, 2, 1), ("s", "yb", 0, 0, 2), ("s", "zb", 0, 3, 1), ("w", "zb", 1, 2, 1), ("s", "zb", 1, 3, 1),
-    ("s", "yb", 0, 14, 2), ("w", "za", 3, 0, 1), ("w", "za", 3, 1, 1), ("s", "za", 3, 0, 2), ("s", "za", 3, 1, 2),
-    ("w", "za", 1, 0, 1), ("w", "ya", 2), ("s", "za", 2, 0, 1), ("s", "za", 2, 1, 1), ("w", "yb", 1, 1, 2),
-    ("w", "za", 1, 1, 1), ("s", "za", 1, 0, 2), ("s", "za", 1, 1, 2), ("w", "za", 0, 1, 2), ("w", "za", 0, 0, 2),
-    ("s", "yb", 0, 2, 2), ("s", "yb", 1, 14, 2), ("w", "zb", 0, 3, 0), ("s", "za", 0, 1, 3), ("s", "zb", 0, 4, 0),
-    ("s", "za", 0, 0, 3), ("w", "zb", 1, 3, 0), ("w", "yb", 1, 15, 2), ("s", "yb", 0, 15, 2), ("s", "yb", 2, 15, 2),
-    ("s", "zb", 1, 4, 0), ("w", "zb", 1, 3, 1), ("w", "zb", 0, 3, 1), ("s", "zb", 0, 4, 1), ("s", "zb", 1, 4, 1),
-    ("w", "za", 3, 1, 2), ("s", "za", 3, 1, 3), ("w", "za", 2, 0, 1), ("s", "za", 2, 0, 2), ("s", "yb", 0, 13, 2),
-    ("s", "yb", 2, 1, 2), ("w", "za", 3, 0, 2), ("w", "za", 1, 0, 2), ("s", "za", 3, 0, 3), ("w", "za", 2, 1, 1),
-    ("w", "yb", 0, 0, 2), ("s", "za", 2, 1, 2), ("w", "za", 1, 1, 2), ("s", "za", 1, 0, 3), ("s", "yb", 1, 3, 2),
-    ("s", "za", 1, 1, 3), ("s", "yb", 1, 13, 2), ("w", "zb", 0, 4, 0), ("s", "zb", 0, 5, 0), ("s", "yb", 2, 0, 2),
-    ("w", "zb", 1, 4, 0), ("s", "zb", 1, 5, 0), ("w", "za", 0, 0, 3), ("w", "zb", 0, 4, 1), ("s", "zb", 0, 5, 1),
-    ("s", "za", 0, 0, 4), ("s", "yb", 1, 2, 2), ("w", "za", 0, 1, 3), ("w", "zb", 1, 4, 1), ("s", "zb", 1, 5, 1),
-    ("s", "za", 0, 1, 4), ("s", "yb", 0, 4, 2), ("w", "za", 2, 0, 2), ("s", "za", 2, 0, 3), ("w", "za", 2, 1, 2),
-    ("w", "za", 3, 0, 3), ("s", "za", 2, 1, 3), ("s", "za", 3, 0, 4), ("s", "yb", 0, 3, 2), ("w", "za", 3, 1, 3),
-    ("s", "za", 3, 1, 4), ("w", "yb", 0, 2, 2), ("s", "yb", 0, 12, 2), ("w", "za", 1, 0, 3), ("s", "yb", 1, 4, 2),
-    ("w", "yb", 0, 14, 2), ("s", "za", 1, 0, 4), ("w", "za", 1, 1, 3), ("s", "za", 1, 1, 4), ("w", "zb", 0, 5, 0),
-    ("s", "zb", 0, 6, 0), ("w", "yb", 0, 1, 2), ("w", "zb", 1, 5, 0), ("s", "zb", 1, 6, 0), ("w", "zb", 0, 5, 1),
-    ("s", "yb", 1, 12, 2), ("s", "zb", 0, 6, 1), ("s", "yb", 2, 2, 2), ("w", "zb", 1, 5, 1), ("s", "zb", 1, 6, 1),
-    ("w", "za", 0, 0, 4), ("w", "yb", 2, 0, 2), ("s", "za", 0, 0, 5), ("s", "yb", 2, 14, 2), ("w", "za", 0, 1, 4),
-    ("s", "za", 0, 1, 5), ("w", "yb", 2, 15, 2), ("w", "yb", 1, 3, 2), ("s", "yb", 1, 5, 2), ("s", "yb", 0, 5, 2),
-    ("w", "za", 2, 0, 3), ("s", "za", 2, 0, 4), ("w", "za", 2, 1, 3), ("s", "za", 2, 1, 4), ("w", "za", 3, 0, 4),
-    ("w", "za", 1, 0, 4), ("s", "za", 1, 0, 5), ("s", "yb", 2, 3, 2), ("w", "za", 3, 1, 4), ("w", "za", 1, 1, 4),
-    ("s", "za", 3, 0, 5), ("w", "yb", 0, 12, 2), ("s", "za", 1, 1, 5), ("s", "za", 3, 1, 5), ("s", "yb", 1, 11, 2),
-    ("w", "yb", 0, 3, 2), ("w", "zb", 0, 6, 0), ("s", "yb", 2, 12, 2), ("w", "yb", 2, 1, 2), ("w", "yb", 1, 14, 2),
-    ("w", "zb", 1, 6, 0), ("s", "zb", 0, 7, 0), ("s", "zb", 1, 7, 0), ("w", "yb", 0, 15, 2), ("w", "zb", 0, 6, 1),
-    ("w", "zb", 1, 6, 1), ("s", "yb", 1, 10, 2), ("s", "zb", 0, 7, 1), ("w", "yb", 1, 13, 2), ("s", "zb", 1, 7, 1),
-    ("w", "yb", 1, 2, 2), ("s", "yb", 1, 6, 2), ("w", "za", 0, 0, 5), ("s", "yb", 2, 13, 2), ("s", "yb", 0, 6, 2),
-    ("w", "za", 2, 0, 4), ("s", "za", 2, 0, 5), ("s", "yb", 0, 10, 2), ("w", "za", 2, 1, 4), ("s", "za", 2, 1, 5),
-    ("s", "za", 0, 0, 6), ("g", 15), ("w", "za", 0, 1, 5), ("s", "za", 0, 1, 6), ("w", "yb", 1, 12, 2),
-    ("s", "yb", 0, 11, 2), ("w", "yb", 0, 4, 2), ("w", "za", 1, 0, 5), ("s", "za", 1, 0, 6), ("w", "za", 1, 1, 5),
-    ("s", "za", 1, 1, 6), ("w", "yb", 1, 5, 2), ("w", "yb", 2, 2, 2), ("g", 2), ("w", "za", 3, 0, 5),
-    ("w", "yb", 2, 3, 2), ("s", "za", 3, 0, 6), ("w", "za", 3, 1, 5), ("s", "za", 3, 1, 6), ("s", "yb", 2, 4, 2),
-    ("s", "yb", 2, 5, 2), ("w", "zb", 1, 7, 0), ("w", "yb", 1, 4, 2), ("s", "zb", 1, 8, 0), ("w", "zb", 0, 7, 1),
-    ("s", "zb", 0, 8, 1), ("g", 3), ("w", "za", 2, 0, 5), ("s", "za", 2, 0, 6), ("w", "zb", 1, 7, 1),
-    ("w", "za", 2, 1, 5), ("s", "yb", 1, 9, 2), ("s", "za", 2, 1, 6), ("w", "yb", 0, 6, 2), ("w", "yb", 1, 11, 2),
-    ("s", "yb", 0, 9, 2), ("w", "za", 0, 0, 6), ("w", "zb", 0, 7, 0), ("w", "za", 0, 1, 6), ("s", "yb", 1, 7, 2),
-    ("s", "yb", 2, 6, 2), ("w", "yb", 1, 0, 2), ("w", "yb", 2, 14, 2), ("s", "za", 0, 1, 7), ("g", 0),
-    ("w", "yb", 0, 5, 2), ("w", "za", 1, 1, 6), ("w", "yb", 2, 12, 2), ("w", "za", 1, 0, 6), ("s", "za", 1, 1, 7),
-    ("s", "za", 1, 0, 7), ("g", 14), ("w", "za", 3, 1, 6), ("w", "za", 3, 0, 6), ("s", "za", 3, 0, 7),
-    ("s", "yb", 2, 11, 2), ("w", "yb", 1, 10, 2), ("w", "yb", 0, 13, 2), ("s", "za", 3, 1, 7), ("w", "yb", 1, 6, 2),
-    ("w", "zb", 1, 8, 0), ("w", "yb", 2, 13, 2), ("w", "zb", 0, 8, 1), ("s", "za", 0, 0, 7), ("s", "yb", 0, 8, 2),
-    ("s", "yb", 1, 8, 2), ("w", "yb", 0, 10, 2), ("g", 12), ("s", "yb", 2, 10, 2), ("w", "za", 2, 0, 6),
-    ("w", "za", 2, 1, 6), ("s", "za", 2, 0, 7), ("w", "yb", 2, 4, 2), ("g", 4), ("w", "yb", 2, 5, 2),
-    ("s", "za", 2, 1, 7), ("s", "yb", 0, 7, 2), ("w", "yb", 1, 9, 2), ("s", "yb", 2, 9, 2), ("g", 13), ("g", 5),
-    ("w", "za", 0, 1, 7), ("w", "yb", 0, 9, 2), ("w", "yb", 1, 7, 2), ("w", "za", 1, 1, 7), ("s", "za", 1, 1, 8),
-    ("s", "za", 0, 1, 8), ("s", "yb", 2, 7, 2), ("w", "yb", 2, 6, 2), ("w", "za", 3, 0, 7), ("s", "za", 3, 0, 8),
-    ("w", "za", 1, 0, 7), ("g", 6), ("w", "yb", 0, 8, 2), ("s", "yb", 2, 8, 2), ("w", "za", 2, 0, 7),
-    ("s", "za", 2, 0, 8), ("w", "za", 0, 0, 7), ("w", "za", 3, 1, 7), ("w", "yb", 2, 11, 2), ("w", "yb", 0, 11, 2),
-    ("g", 1), ("w", "yb", 2, 10, 2), ("g", 10), ("w", "za", 2, 1, 7), ("g", 11), ("w", "yb", 2, 9, 2), ("g", 9),
-    ("w", "yb", 0, 7, 2), ("w", "yb", 1, 8, 2), ("w", "za", 3, 0, 8), ("w", "za", 1, 1, 8), ("w", "yb", 2, 7, 2),
-    ("g", 7), ("w", "za", 0, 1, 8), ("w", "yb", 2, 8, 2), ("w", "za", 2, 0, 8), ("g", 8),
+    ("s", "zb", 0, 1, 0), ("s", "ya", 1), ("s", "ya", 3), ("s", "zb", 1, 1, 0), ("s", "zb", 1, 1, 1), ("s", "ya", 2),
+    ("s", "zb", 0, 1, 1), ("s", "za", 0, 1, 1), ("s", "za", 0, 0, 1), ("w", "zb", 0, 1, 0), ("s", "zb", 0, 2, 0),
+    ("w", "zb", 0, 1, 1), ("s", "zb", 0, 2, 1), ("w", "zb", 1, 1, 0), ("s", "zb", 1, 2, 0), ("w", "ya", 1),
+    ("s", "za", 3, 0, 1), ("w", "zb", 1, 1, 1), ("w", "za", 0, 0, 1), ("s", "yb", 1, 1, 2), ("s", "za", 0, 0, 2),
+    ("s", "zb", 1, 2, 1), ("s", "za", 3, 1, 1), ("w", "ya", 3), ("s", "za", 1, 0, 1), ("s", "yb", 1, 15, 2),
+    ("s", "yb", 0, 15, 2), ("w", "za", 0, 1, 1), ("s", "za", 0, 1, 2), ("s", "za", 1, 1, 1), ("w", "zb", 0, 2, 0),
+    ("s", "zb", 0, 3, 0), ("w", "zb", 1, 2, 0), ("s", "yb", 0, 0, 2), ("s", "zb", 1, 3, 0), ("w", "zb", 0, 2, 1),
+    ("s", "zb", 0, 3, 1), ("w", "za", 3, 0, 1), ("w", "zb", 1, 2, 1), ("s", "za", 3, 0, 2), ("s", "zb", 1, 3, 1),
+    ("w", "za", 3, 1, 1), ("s", "za", 3, 1, 2), ("w", "ya", 2), ("s", "za", 2, 0, 1), ("s", "yb", 1, 0, 2),
+    ("s", "za", 2, 1, 1), ("s", "yb", 1, 14, 2), ("s", "yb", 1, 2, 2), ("s", "yb", 0, 14, 2), ("w", "za", 0, 1, 2),
+    ("w", "za", 1, 1, 1), ("w", "za", 1, 0, 1), ("s", "za", 1, 0, 2), ("w", "za", 0, 0, 2), ("s", "za", 1, 1, 2),
+    ("w", "yb", 1, 1, 2), ("s", "za", 0, 0, 3), ("w", "zb", 0, 3, 0), ("s", "yb", 0, 1, 2), ("s", "yb", 0, 2, 2),
+    ("s", "zb", 0, 4, 0), ("s", "za", 0, 1, 3), ("w", "zb", 1, 3, 0), ("s", "zb", 1, 4, 0), ("w", "zb", 0, 3, 1),
+    ("s", "zb", 0, 4, 1), ("w", "yb", 1, 15, 2), ("s", "yb", 2, 15, 2), ("w", "zb", 1, 3, 1), ("w", "yb", 0, 0, 2),
+    ("s", "zb", 1, 4, 1), ("s", "yb", 0, 13, 2), ("w", "za", 2, 0, 1), ("s", "za", 2, 0, 2), ("w", "za", 3, 1, 2),
+    ("w", "za", 3, 0, 2), ("s", "za", 3, 1, 3), ("w", "za", 2, 1, 1), ("s", "yb", 1, 3, 2), ("s", "za", 3, 0, 3),
+    ("s", "yb", 1, 13, 2), ("s", "za", 2, 1, 2), ("w", "za", 1, 0, 2), ("s", "za", 1, 0, 3), ("w", "yb", 1, 0, 2),
+    ("w", "za", 1, 1, 2), ("s", "za", 1, 1, 3), ("s", "yb", 0, 3, 2), ("w", "za", 0, 1, 3), ("w", "za", 0, 0, 3),
+    ("w", "zb", 0, 4, 0), ("s", "zb", 0, 5, 0), ("w", "zb", 1, 4, 0), ("s", "zb", 1, 5, 0), ("w", "zb", 0, 4, 1),
+    ("s", "zb", 0, 5, 1), ("w", "zb", 1, 4, 1), ("s", "zb", 1, 5, 1), ("s", "za", 0, 1, 4), ("s", "za", 0, 0, 4),
+    ("s", "yb", 0, 12, 2), ("w", "za", 2, 0, 2), ("s", "za", 2, 0, 3), ("w", "za", 2, 1, 2), ("s", "za", 2, 1, 3),
+    ("w", "yb", 0, 2, 2), ("s", "yb", 1, 12, 2), ("s", "yb", 0, 4, 2), ("w", "yb", 2, 15, 2), ("w", "za", 3, 0, 3),
+    ("w", "za", 3, 1, 3), ("s", "za", 3, 0, 4), ("s", "za", 3, 1, 4), ("w", "za", 1, 0, 3), ("s", "yb", 2, 1, 2),
+    ("w", "yb", 1, 3, 2), ("w", "za", 1, 1, 3), ("s", "za", 1, 0, 4), ("w", "yb", 1, 2, 2), ("s", "yb", 2, 3, 2),
+    ("s", "za", 1, 1, 4), ("w", "zb", 0, 5, 0), ("w", "yb", 0, 14, 2), ("s", "zb", 0, 6, 0), ("s", "yb", 2, 0, 2),
+    ("w", "zb", 1, 5, 0), ("s", "zb", 1, 6, 0), ("w", "zb", 0, 5, 1), ("s", "yb", 2, 2, 2), ("s", "zb", 0, 6, 1),
+    ("w", "zb", 1, 5, 1), ("w", "za", 0, 0, 4), ("s", "zb", 1, 6, 1), ("w", "za", 0, 1, 4), ("s", "za", 0, 0, 5),
+    ("s", "yb", 1, 5, 2), ("s", "za", 0, 1, 5), ("s", "yb", 0, 5, 2), ("w", "za", 2, 0, 3), ("s", "za", 2, 0, 4),
+    ("s", "yb", 1, 11, 2), ("w", "za", 2, 1, 3), ("s", "za", 2, 1, 4), ("w", "za", 3, 1, 4), ("w", "za", 3, 0, 4),
+    ("s", "yb", 2, 14, 2), ("w", "za", 1, 0, 4), ("s", "za", 1, 0, 5), ("s", "za", 3, 1, 5), ("s", "za", 3, 0, 5),
+    ("w", "za", 1, 1, 4), ("s", "za", 1, 1, 5), ("s", "yb", 1, 4, 2), ("w", "zb", 0, 6, 0), ("w", "zb", 1, 6, 0),
+    ("w", "yb", 0, 4, 2), ("s", "zb", 1, 7, 0), ("w", "yb", 0, 3, 2), ("w", "zb", 0, 6, 1), ("s", "yb", 0, 6, 2),
+    ("w", "zb", 1, 6, 1), ("s", "zb", 0, 7, 1), ("s", "yb", 1, 6, 2), ("w", "yb", 0, 15, 2), ("w", "yb", 0, 12, 2),
+    ("s", "yb", 0, 10, 2), ("s", "zb", 1, 7, 1), ("s", "zb", 0, 7, 0), ("w", "yb", 2, 2, 2), ("w", "yb", 2, 3, 2),
+    ("w", "za", 2, 0, 4), ("s", "za", 2, 0, 5), ("w", "za", 0, 0, 5), ("w", "yb", 1, 14, 2), ("w", "za", 2, 1, 4),
+    ("s", "za", 2, 1, 5), ("s", "za", 0, 0, 6), ("w", "za", 0, 1, 5), ("w", "yb", 1, 5, 2), ("s", "yb", 2, 12, 2),
+    ("s", "yb", 2, 4, 2), ("s", "yb", 1, 10, 2), ("g", 15), ("w", "yb", 2, 1, 2), ("w", "za", 1, 0, 5),
+    ("s", "za", 1, 0, 6), ("s", "za", 0, 1, 6), ("s", "yb", 0, 11, 2), ("s", "yb", 2, 5, 2), ("w", "za", 3, 0, 5),
+    ("s", "za", 3, 0, 6), ("w", "yb", 1, 13, 2), ("w", "za", 1, 1, 5), ("s", "za", 1, 1, 6), ("g", 2),
+    ("w", "yb", 2, 0, 2), ("w", "yb", 0, 5, 2), ("w", "za", 3, 1, 5), ("s", "za", 3, 1, 6), ("s", "yb", 2, 13, 2),
+    ("w", "zb", 1, 7, 0), ("s", "zb", 1, 8, 0), ("w", "zb", 0, 7, 1), ("s", "zb", 0, 8, 1), ("g", 3),
+    ("w", "zb", 1, 7, 1), ("s", "yb", 1, 9, 2), ("w", "yb", 1, 6, 2), ("w", "zb", 0, 7, 0), ("w", "yb", 0, 6, 2),
+    ("s", "yb", 2, 6, 2), ("w", "za", 2, 1, 5), ("s", "za", 2, 1, 6), ("w", "za", 2, 0, 5), ("s", "za", 2, 0, 6),
+    ("w", "yb", 2, 14, 2), ("s", "yb", 1, 7, 2), ("g", 0), ("w", "za", 0, 0, 6), ("s", "yb", 0, 9, 2),
+    ("w", "za", 0, 1, 6), ("s", "za", 0, 1, 7), ("w", "yb", 0, 10, 2), ("s", "za", 0, 0, 7), ("g", 14),
+    ("w", "yb", 1, 11, 2), ("w", "za", 1, 0, 6), ("w", "za", 1, 1, 6), ("s", "za", 1, 1, 7), ("w", "yb", 1, 12, 2),
+    ("s", "yb", 2, 11, 2), ("w", "za", 3, 0, 6), ("w", "yb", 2, 4, 2), ("w", "za", 3, 1, 6), ("s", "za", 3, 0, 7),
+    ("w", "yb", 2, 12, 2), ("w", "zb", 0, 8, 1), ("w", "zb", 1, 8, 0), ("s", "yb", 0, 8, 2), ("s", "yb", 1, 8, 2),
+    ("w", "yb", 1, 4, 2), ("s", "za", 3, 1, 7), ("w", "za", 2, 0, 6), ("w", "yb", 2, 5, 2), ("g", 5),
+    ("s", "yb", 2, 10, 2), ("w", "yb", 2, 13, 2), ("g", 12), ("w", "yb", 0, 13, 2), ("w", "yb", 1, 9, 2),
+    ("w", "yb", 0, 11, 2), ("s", "za", 1, 0, 7), ("s", "yb", 2, 9, 2), ("w", "za", 2, 1, 6), ("s", "za", 2, 0, 7),
+    ("w", "yb", 2, 6, 2), ("s", "za", 2, 1, 7), ("s", "yb", 0, 7, 2), ("g", 13), ("w", "za", 0, 1, 7),
+    ("w", "yb", 1, 7, 2), ("s", "za", 0, 1, 8), ("s", "yb", 2, 7, 2), ("g", 4), ("w", "za", 1, 1, 7),
+    ("s", "za", 1, 1, 8), ("w", "za", 3, 0, 7), ("s", "za", 3, 0, 8), ("w", "yb", 0, 1, 2), ("w", "yb", 1, 10, 2),
+    ("w", "yb", 0, 8, 2), ("s", "yb", 2, 8, 2), ("w", "za", 2, 0, 7), ("s", "za", 2, 0, 8), ("w", "yb", 0, 9, 2),
+    ("g", 1), ("w", "yb", 1, 8, 2), ("w", "yb", 2, 11, 2), ("g", 11), ("g", 6), ("w", "yb", 2, 10, 2),
+    ("w", "za", 0, 0, 7), ("g", 10), ("w", "yb", 2, 9, 2), ("w", "za", 3, 1, 7), ("w", "za", 2, 1, 7),
+    ("w", "za", 1, 0, 7), ("g", 9), ("w", "yb", 0, 7, 2), ("w", "yb", 2, 7, 2), ("g", 7), ("w", "za", 0, 1, 8),
+    ("w", "za", 1, 1, 8), ("w", "za", 3, 0, 8), ("w", "yb", 2, 8, 2), ("w", "za", 2, 0, 8), ("g", 8),
 )
 
 

time: 98 us -> 99.1 us (1.011)
  Pallas kernels: 95.7 us -> 96.8 us
    pallas_call x1, Pallas kernels: 95.7 us -> 96.8 us  [body(): pl.pallas_call(kernel, out_shape=jax.ShapeDtypeStruct((B, F), jnp.bfloat1...]
where the time goes in v5:
time: 99.1 us; the launch traced here: 99 us
  Pallas kernels  96.8 us (98%)
  local copies, waits for them, and re-layouts  1.47 us (1%)
    pallas_call x1, Pallas kernels, body(): pl.pallas_call(kernel, out_shape=jax.ShapeDtypeStruct((B, F), jnp.bfloat1...  96.8 us

profile of v5, /device:TPU:1, one launch (start us, length us, event | category | flops | bytes accessed | tf_op | source)
XLA Modules:
  0.0 99.0 jit_solution(2837937193092104937)
XLA Ops:
  0.7 96.8 %shard_map.73 = bf16[128,256]{1,0:T(8,128)(2,1)} custom-call(bf16[128,256]{1,0:T(8,128)(2,1)} %features.1, bf16[96,128,128]{2,1,0:T(8,128)(2,1)} %tiles_hbm.1, s32[1,96]{1,0:T(1,128)} %bitcast.2, s32[1,96]{1,0:T(1,128)} %bitcast.3, s32[1]{0:T(128)S(6)} %copy.9.count_ref, bf16[2,256,256]{2,1,0:T(8,128)(2,1)} %weights_hbm.1, f32[2,256]{1,0:T(2,128)} %biases_hbm.1), custom_call_target="tpu_custom_call" | custom-call | flops 8589934592 | bytes 4194304 | tf_op jit(solution)/shard_map/pallas_call | solution.py:355
  97.5 1.5 %copy.10 = bf16[128,256]{1,0:T(8,128)(2,1)} copy(bf16[128,256]{1,0:T(8,128)(2,1)} %shard_map.73) | data formatting | bytes 131072
